TPU v7x, 32 devices: a whole 2x2x4 slice. The times are simulated.
32 devices in a mesh: dp: 2 (over y), expert: 16 (over z, x, core).
Axes of the slice: x: 2, y: 2, z: 4, core: 2. Of those that a mesh axis runs over, the one named last changes fastest.
Arguments:
- tokens: bfloat16 [1024, 2048], P(('dp', 'expert')), may hold values from -6 to 6
- routes: int32 [1024, 8], P(('dp', 'expert')), may hold values from 0 to 15, all different within a row; in each aligned block of 32 rows (0 to 31, 32 to 63, ...) at most 24 rows name the same one
- gates: float32 [1024, 8], P(('dp', 'expert')), may hold values from 0.1 to 0.6
- w_gate: bfloat16 [16, 2048, 768], P('expert'), may hold values from -0.125 to 0.125
- w_up: bfloat16 [16, 2048, 768], P('expert'), may hold values from -0.125 to 0.125
- w_down: bfloat16 [16, 768, 2048], P('expert'), may hold values from -0.21875 to 0.21875
- swap_flags: int32 [16], replicated, may hold values from 0 to 1, as said below
- d_out: bfloat16 [1024, 2048], P(('dp', 'expert')), may hold values from -6 to 6
Outputs:
- mixture: bfloat16 [1024, 2048], P(('dp', 'expert'))
- d_tokens: bfloat16 [1024, 2048], P(('dp', 'expert'))
- d_gates: float32 [1024, 8], P(('dp', 'expert'))
- g_gate: bfloat16 [16, 2048, 768], P('expert', 'dp')
- g_up: bfloat16 [16, 2048, 768], P('expert', 'dp')
- g_down: bfloat16 [16, 768, 2048], P('expert', None, 'dp')
Inputs may be any that keep to these rules, and one draw needn't show every extreme that they name: `routes`: among the 32 rows of one device no expert is named more than 24 times, and in every draw some device names some expert exactly 24 times. swap_flags[i] equals swap_flags[i + 8]; swap_flags[0] and swap_flags[7] are 1.
All inputs are finite; a program needn't handle non-finite values.
Results may differ from a plain program's by a relative error of at most 0.0095.
Values may be sent and summed in bfloat16 or wider, within the bound.
A program may use at most 128 MiB of HBM per device.

v0:
```python
import jax
import jax.numpy as jnp
from jax import lax
from jax.sharding import PartitionSpec as P


def from_partner(value, axis, stride):
    return lax.ppermute(value, axis, [(i, i ^ 1 << stride) for i in range(lax.axis_size(axis))])


def slot_tables(target, expert_count, capacity):
    pair_count = target.shape[0]
    onehot = (target[:, None] == jnp.arange(expert_count, dtype=jnp.int32)[None, :]).astype(
        jnp.int32
    )
    before = jnp.cumsum(onehot, axis=0) - onehot
    position = jnp.sum(onehot * before, axis=1)
    slot_index = target * capacity + position
    matches = slot_index[None, :] == jnp.arange(expert_count * capacity, dtype=jnp.int32)[:, None]
    alive = jnp.any(matches, axis=1)
    source = jnp.sum(
        jnp.where(matches, jnp.arange(pair_count, dtype=jnp.int32)[None, :], 0), axis=1
    )
    return (slot_index, alive, source)


def contract_rows(left, right):
    return lax.dot_general(
        left, right, (((0,), (0,)), ((), ())), preferred_element_type=jnp.float32
    )


def contract_cols(left, right):
    return lax.dot_general(
        left, right, (((1,), (1,)), ((), ())), preferred_element_type=jnp.float32
    )


def on_device(tokens, routes, gates, w_gate, w_up, w_down, swap_flags, d_out):
    expert_count = lax.axis_size("expert")
    pair_bit = expert_count.bit_length() - 2
    own_index = lax.axis_index("expert")
    tok_count, model_width = tokens.shape
    top_count = routes.shape[1]
    hidden_width = w_gate.shape[2]
    capacity = min(
        tok_count, (3 * tok_count * top_count + 2 * expert_count - 1) // (2 * expert_count)
    )
    own_flag = swap_flags[own_index]
    weights = (w_gate[0], w_up[0], w_down[0])
    routed = routes.reshape(-1)
    gate_mat, up_mat, down_mat = weights
    slot_index, alive, source = slot_tables(routed, expert_count, capacity)
    outbound = jnp.where(
        alive[:, None], tokens[source // top_count], jnp.zeros((), jnp.bfloat16)
    ).reshape(expert_count, capacity, model_width)
    items = lax.all_to_all(outbound, "expert", split_axis=0, concat_axis=0, tiled=True)
    many = items.shape[1]
    expert_rows_in = items.reshape(-1, model_width)
    pre_gate = jnp.dot(expert_rows_in, gate_mat, preferred_element_type=jnp.float32)
    pre_up = jnp.dot(expert_rows_in, up_mat, preferred_element_type=jnp.float32)
    expert_hidden = (pre_gate * jax.nn.sigmoid(pre_gate) * pre_up).astype(jnp.bfloat16)
    result = jnp.dot(expert_hidden, down_mat, preferred_element_type=jnp.float32).astype(
        jnp.bfloat16
    )
    result, pre_gate, pre_up, received = (
        result.reshape(expert_count, many, model_width),
        pre_gate.reshape(expert_count, many, hidden_width),
        pre_up.reshape(expert_count, many, hidden_width),
        items,
    )
    returned_rows = lax.all_to_all(result, "expert", split_axis=0, concat_axis=0, tiled=True)
    picked = returned_rows.reshape(-1, model_width)[slot_index].reshape(
        tok_count, top_count, model_width
    )
    mixture = jnp.sum(gates[:, :, None] * picked, axis=1).astype(jnp.bfloat16)
    d_gates = jnp.einsum("td,tkd->tk", d_out, picked, preferred_element_type=jnp.float32)
    cot_pairs = (
        (gates[:, :, None] * d_out.astype(jnp.float32)[:, None, :])
        .astype(jnp.bfloat16)
        .reshape(-1, model_width)
    )
    cot_out = jnp.where(alive[:, None], cot_pairs[source], jnp.zeros((), jnp.bfloat16)).reshape(
        expert_count, capacity, model_width
    )
    cot_rows = lax.all_to_all(cot_out, "expert", split_axis=0, concat_axis=0, tiled=True).reshape(
        -1, model_width
    )
    gate_rows = pre_gate.reshape(-1, hidden_width)
    up_rows = pre_up.reshape(-1, hidden_width)
    rows_in = received.reshape(-1, model_width)
    logistic = jax.nn.sigmoid(gate_rows)
    activated = gate_rows * logistic
    hidden = (activated * up_rows).astype(jnp.bfloat16)
    d_hidden = contract_cols(cot_rows, down_mat)
    grad_gate_pre = (d_hidden * up_rows * logistic * (1.0 + gate_rows * (1.0 - logistic))).astype(
        jnp.bfloat16
    )
    grad_up_pre = (d_hidden * activated).astype(jnp.bfloat16)
    d_rows = (contract_cols(grad_gate_pre, gate_mat) + contract_cols(grad_up_pre, up_mat)).astype(
        jnp.bfloat16
    )
    back_rows = lax.all_to_all(
        d_rows.reshape(expert_count, capacity, model_width),
        "expert",
        split_axis=0,
        concat_axis=0,
        tiled=True,
    )
    d_tokens = jnp.sum(
        back_rows.reshape(-1, model_width)[slot_index]
        .reshape(tok_count, top_count, model_width)
        .astype(jnp.float32),
        axis=1,
    ).astype(jnp.bfloat16)
    gate_up_grads = jnp.concatenate([grad_gate_pre, grad_up_pre], axis=1)
    grads = lax.psum_scatter(
        jnp.concatenate(
            [contract_rows(rows_in, gate_up_grads), contract_rows(cot_rows, hidden)], axis=1
        ).astype(jnp.bfloat16),
        "dp",
        scatter_dimension=0,
        tiled=True,
    ).astype(jnp.float32)
    g_gate = grads[:, :hidden_width].astype(jnp.bfloat16)[None]
    g_up = grads[:, hidden_width : 2 * hidden_width].astype(jnp.bfloat16)[None]
    g_down = grads[:, 2 * hidden_width :].T.astype(jnp.bfloat16)[None]
    traded = from_partner((g_gate, g_up, g_down), "expert", pair_bit)
    g_gate, g_up, g_down = tuple(
        (
            jnp.where(own_flag == 1, other, mine)
            for other, mine in zip(traded, (g_gate, g_up, g_down))
        )
    )
    return (mixture, d_tokens, d_gates, g_gate, g_up, g_down)


def solution(mesh):
    return jax.shard_map(
        on_device,
        mesh=mesh,
        in_specs=(
            P(("dp", "expert"), None),
            P(("dp", "expert"), None),
            P(("dp", "expert"), None),
            P("expert", None, None),
            P("expert", None, None),
            P("expert", None, None),
            P(),
            P(("dp", "expert"), None),
        ),
        out_specs=(
            P(("dp", "expert"), None),
            P(("dp", "expert"), None),
            P(("dp", "expert"), None),
            P("expert", "dp", None),
            P("expert", "dp", None),
            P("expert", None, "dp"),
        ),
        check_vma=False,
    )
```

profile of v0, /device:TPU:0, one launch (start us, length us, event | category | flops | bytes accessed | tf_op | source)
XLA Modules:
  0.0 467.6 jit_solution(1973795815836985657)
XLA Ops:
  7.2 0.0 copy-start
  7.2 0.9 copy.26
  8.1 0.1 reshape.182
  8.2 0.1 eq.47
  8.3 0.6 reduce-window.6
  8.9 0.2 slice_reduce_fusion
  9.1 0.1 fusion.28
  9.2 0.2 select_reduce_fusion
  9.4 0.2 fusion.24
  9.5 0.9 convert_element_type.52
  10.4 0.8 copy.25
  11.2 0.1 mul.86
  11.3 0.1 broadcast_in_dim.52
  11.4 1.2 fusion.17
  12.6 6.4 %gather_fusion.2 = bf16[384,2048]{1,0:T(8,128)(2,1)} fusion(bf16[256,2048]{1,0:T(8,128)(2,1)} %fusion.17, s32[1024]{0:T(1024)S(1)} %get-tuple-element.36), kind=kCustom, calls=%fused_computation.2 | custom fusion | bytes 3147264 | tf_op jit(solution)/shard_map/gather | solution.py:83
  19.0 0.0 copy-done.1
  19.0 3.1 gather_fusion
  22.1 3.3 broadcast_select_fusion.3
  25.4 43.3 %all_to_all.20 = bf16[16,24,2048]{2,1,0:T(8,128)(2,1)} all-to-all(bf16[16,24,2048]{2,1,0:T(8,128)(2,1)S(1)} %get-tuple-element.34), channel_id=1, replica_groups=mesh['dp'=2,'expert'=16] {'expert'}, dimensions={0} | all-to-all | bytes 3145728 | tf_op jit(solution)/shard_map/all_to_all | solution.py:86
  68.8 5.1 %all-to-all-start = ((bf16[16,24,2048]{2,1,0:T(8,128)(2,1)}), bf16[16,24,2048]{2,1,0:T(8,128)(2,1)}, u32[]{:S(2)}, u32[]{:S(2)}) async-start(bf16[16,24,2048]{2,1,0:T(8,128)(2,1)} %get-tuple-element.35), calls=%async_computation | async-start | bytes 3145728 | tf_op jit(solution)/shard_map/all_to_all | solution.py:57
  73.9 0.2 reduce-scatter.2.cloned.1.call-start
  74.1 4.8 %fusion = f32[384,768]{1,0:T(8,128)} fusion(bf16[384,2048]{1,0:T(8,128)(2,1)} %bitcast.89, bf16[1,768,2048]{2,1,0:T(8,128)(2,1)} %param.13), kind=kOutput, calls=%fused_computation.7 | convolution fusion | flops 1207959552 | bytes 5898240 | tf_op jit(solution)/shard_map/dot_general | solution.py:34
  78.9 27.0 %all-to-all-done = bf16[16,24,2048]{2,1,0:T(8,128)(2,1)} async-done(((bf16[16,24,2048]{2,1,0:T(8,128)(2,1)}), bf16[16,24,2048]{2,1,0:T(8,128)(2,1)}, u32[]{:S(2)}, u32[]{:S(2)}) %all-to-all-start) | async-done | bytes 1572896 | tf_op jit(solution)/shard_map/all_to_all | solution.py:57
  105.9 3.8 fusion.6
  109.8 3.3 multiply_convert_fusion.1
  113.1 0.0 copy-start.9
  113.1 0.0 copy-start.11
  113.1 0.0 copy-done.3
  113.2 1.9 convolution_convert_fusion.1
  115.1 5.2 %convolution_convert_fusion = bf16[2048,1536]{0,1:T(8,128)(2,1)S(1)} fusion(bf16[384,2048]{1,0:T(8,128)(2,1)} %bitcast.2, bf16[384,768]{1,0:T(8,128)(2,1)S(1)} %get-tuple-element.32, bf16[384,768]{1,0:T(8,128)(2,1)S(1)} %get-tuple-element.31), kind=kOutput, calls=%fused_computation.5 | convolution fusion | flops 2421424128 | bytes 9043968 | tf_op jit(solution)/shard_map/dot_general | solution.py:28
  120.2 11.6 %pad_maximum_fusion = bf16[2048,2304]{0,1:T(8,128)(2,1)} fusion(bf16[2048,768]{0,1:T(8,128)(2,1)S(1)} %convolution_convert_fusion.1, bf16[2048,1536]{0,1:T(8,128)(2,1)S(1)} %convolution_convert_fusion), kind=kLoop, calls=%fused_computation.4 | loop fusion | flops 18874368 | bytes 18874368 | tf_op jit(solution)/shard_map/concatenate | solution.py:118
  131.8 0.0 reduce-scatter.2.cloned.1.call-update
  131.8 4.6 fusion.14
  136.4 9.2 %all-to-all-start.1 = ((bf16[16,24,2048]{2,1,0:T(8,128)(2,1)}), bf16[16,24,2048]{2,1,0:T(8,128)(2,1)}, u32[]{:S(2)}, u32[]{:S(2)}) async-start(bf16[16,24,2048]{2,1,0:T(8,128)(2,1)} %bitcast.91), calls=%async_computation.1 | async-start | bytes 3145728 | tf_op jit(solution)/shard_map/all_to_all | solution.py:72
  145.6 3.5 fusion.4
  149.2 0.0 copy-done.8
  149.2 2.6 add_convert_fusion
  151.8 25.9 %all-to-all-done.1 = bf16[16,24,2048]{2,1,0:T(8,128)(2,1)} async-done(((bf16[16,24,2048]{2,1,0:T(8,128)(2,1)}), bf16[16,24,2048]{2,1,0:T(8,128)(2,1)}, u32[]{:S(2)}, u32[]{:S(2)}) %all-to-all-start.1) | async-done | bytes 1572896 | tf_op jit(solution)/shard_map/all_to_all | solution.py:72
  177.7 9.2 %all-to-all-start.3 = ((bf16[16,24,2048]{2,1,0:T(8,128)(2,1)}), bf16[16,24,2048]{2,1,0:T(8,128)(2,1)}, u32[]{:S(2)}, u32[]{:S(2)}) async-start(bf16[16,24,2048]{2,1,0:T(8,128)(2,1)} %bitcast.88), calls=%async_computation.3 | async-start | bytes 3145728 | tf_op jit(solution)/shard_map/all_to_all | solution.py:103
  186.8 0.0 copy-start.5
  186.8 0.0 copy-start.6
  186.8 60.1 %reduce-scatter.2.cloned.1.call-done = bf16[1024,2304]{0,1:T(8,128)(2,1)} async-done(((bf16[2048,2304]{0,1:T(8,128)(2,1)}), bf16[1024,2304]{0,1:T(8,128)(2,1)}) %reduce-scatter.2.cloned.1.call-update) | async-done | bytes 4718608 | tf_op jit(solution)/shard_map/reduce_scatter | solution.py:117
  247.0 4.7 %slice_bitcast_fusion = (bf16[1,768,1024]{2,1,0:T(8,128)(2,1)}, bf16[1,1024,768]{1,2,0:T(8,128)(2,1)}, bf16[1,1024,768]{1,2,0:T(8,128)(2,1)}) fusion(bf16[1024,2304]{0,1:T(8,128)(2,1)} %reduce-scatter.2.cloned.1.call-done), kind=kLoop, calls=%fused_computation.24 | loop fusion | bytes 9437184 | tf_op jit(solution)/shard_map/broadcast_in_dim | solution.py:127
  251.7 2.4 collective-permute-start.1
  254.1 0.5 collective-permute-start
  254.6 2.4 collective-permute-start.2
  257.0 0.1 copy.29
  257.1 0.1 mul.84
  257.2 0.6 dynamic_slice.3
  258.5 5.0 %gather_fusion.1 = bf16[256,2048]{1,0:T(8,128)(2,1)} fusion(bf16[384,2048]{1,0:T(8,128)(2,1)} %bitcast.7, s32[1024]{0:T(1024)S(1)} %pad_clamp_fusion.1), kind=kCustom, calls=%fused_computation.1 | custom fusion | bytes 2098176 | tf_op jit(solution)/shard_map/gather | solution.py:73
  263.4 0.0 all-to-all-done.3
  263.4 5.0 %gather_fusion.3 = bf16[256,2048]{1,0:T(8,128)(2,1)} fusion(bf16[384,2048]{1,0:T(8,128)(2,1)} %bitcast.15, s32[1024]{0:T(1024)S(1)} %pad_clamp_fusion.1), kind=kCustom, calls=%fused_computation.3 | custom fusion | bytes 2098176 | tf_op jit(solution)/shard_map/gather | solution.py:111
  268.4 0.0 copy-done.4
  268.4 2.0 fusion.22
  270.4 0.7 copy.34
  271.1 2.7 bitcast_reduce_fusion
  273.8 1.6 multiply_reduce_fusion
  275.4 115.8 %collective-permute-done.1 = bf16[1,1024,768]{1,2,0:T(8,128)(2,1)} collective-permute-done((bf16[1,1024,768]{1,2,0:T(8,128)(2,1)}, bf16[1,1024,768]{1,2,0:T(8,128)(2,1)}, u32[]{:S(2)}, u32[]{:S(2)}) %collective-permute-start.1) | collective-permute-done | bytes 1572896 | tf_op jit(solution)/shard_map/ppermute | solution.py:8
  391.2 33.7 %collective-permute-done = bf16[1,1024,768]{1,2,0:T(8,128)(2,1)} collective-permute-done((bf16[1,1024,768]{1,2,0:T(8,128)(2,1)}, bf16[1,1024,768]{1,2,0:T(8,128)(2,1)}, u32[]{:S(2)}, u32[]{:S(2)}) %collective-permute-start) | collective-permute-done | bytes 1572896 | tf_op jit(solution)/shard_map/ppermute | solution.py:8
  424.9 4.8 %broadcast_select_fusion.1 = (bf16[1,1024,768]{1,2,0:T(8,128)(2,1)}, bf16[1,1024,768]{1,2,0:T(8,128)(2,1)}) fusion(bf16[1,1024,768]{1,2,0:T(8,128)(2,1)} %collective-permute-done.1, pred[]{:T(512)} %bitcast.19, bf16[1024,2304]{0,1:T(8,128)(2,1)} %reduce-scatter.2.cloned.1.call-done, bf16[1,1024,768]{1,2,0:T(8,128)(2,1)} %collective-permute-done), kind=kLoop, calls=%fused_computation.28 | loop fusion | flops 1572864 | bytes 9437185 | tf_op jit(solution)/shard_map/jit(_where)/select_n | solution.py:131
  429.7 2.6 copy.31
  432.3 2.6 copy.32
  434.8 22.7 %collective-permute-done.2 = bf16[1,768,1024]{2,1,0:T(8,128)(2,1)} collective-permute-done((bf16[1,768,1024]{2,1,0:T(8,128)(2,1)}, bf16[1,768,1024]{2,1,0:T(8,128)(2,1)}, u32[]{:S(2)}, u32[]{:S(2)}) %collective-permute-start.2) | collective-permute-done | bytes 1572896 | tf_op jit(solution)/shard_map/ppermute | solution.py:8
  457.5 3.2 broadcast_select_fusion
  (24 shorter events, 0.1 us)
Async XLA Ops:
  7.2 102.6 %copy-start = (bf16[1,2048,768]{2,1,0:T(8,128)(2,1)S(1)}, bf16[1,2048,768]{2,1,0:T(8,128)(2,1)}, u32[]{:S(2)}) copy-start(bf16[1,2048,768]{2,1,0:T(8,128)(2,1)} %param.11) | copy-start | bytes 9437188
  12.6 6.5 %copy-start.1 = (bf16[32,2048]{1,0:T(8,128)(2,1)S(1)}, bf16[32,2048]{1,0:T(8,128)(2,1)}, u32[]{:S(2)}) copy-start(bf16[32,2048]{1,0:T(8,128)(2,1)} %param.8) | copy-start | bytes 393220
  68.8 37.1 %all-to-all-start = ((bf16[16,24,2048]{2,1,0:T(8,128)(2,1)}), bf16[16,24,2048]{2,1,0:T(8,128)(2,1)}, u32[]{:S(2)}, u32[]{:S(2)}) async-start(bf16[16,24,2048]{2,1,0:T(8,128)(2,1)} %get-tuple-element.35), calls=%async_computation | async-start | bytes 3145728 | tf_op jit(solution)/shard_map/all_to_all | solution.py:57
  73.9 173.1 %reduce-scatter.2.cloned.1.call-start = ((), (), s32[]{:S(2)}) async-start(), calls=%async_computation.5 | async-start | bytes 14155776 | tf_op jit(solution)/shard_map/reduce_scatter | solution.py:117
  105.9 3.9 copy-start.10
  109.8 3.4 copy-start.3
  113.1 1.9 copy-start.9
  113.1 1.9 copy-start.7
  113.1 1.9 copy-start.11
  136.4 41.2 %all-to-all-start.1 = ((bf16[16,24,2048]{2,1,0:T(8,128)(2,1)}), bf16[16,24,2048]{2,1,0:T(8,128)(2,1)}, u32[]{:S(2)}, u32[]{:S(2)}) async-start(bf16[16,24,2048]{2,1,0:T(8,128)(2,1)} %bitcast.91), calls=%async_computation.1 | async-start | bytes 3145728 | tf_op jit(solution)/shard_map/all_to_all | solution.py:72
  145.6 3.6 copy-start.8
  177.7 85.8 %all-to-all-start.3 = ((bf16[16,24,2048]{2,1,0:T(8,128)(2,1)}), bf16[16,24,2048]{2,1,0:T(8,128)(2,1)}, u32[]{:S(2)}, u32[]{:S(2)}) async-start(bf16[16,24,2048]{2,1,0:T(8,128)(2,1)} %bitcast.88), calls=%async_computation.3 | async-start | bytes 3145728 | tf_op jit(solution)/shard_map/all_to_all | solution.py:103
  186.8 70.2 %copy-start.5 = (s32[32,8]{0,1:T(8,128)S(1)}, s32[32,8]{0,1:T(8,128)}, u32[]{:S(2)}) copy-start(s32[32,8]{0,1:T(8,128)} %param.9) | copy-start | bytes 3076
  186.8 70.3 %copy-start.6 = (s32[16]{0:T(128)S(1)}, s32[16]{0:T(128)}, u32[]{:S(2)}) copy-start(s32[16]{0:T(128)} %param.14) | copy-start | bytes 196
  251.7 139.5 %collective-permute-start.1 = (bf16[1,1024,768]{1,2,0:T(8,128)(2,1)}, bf16[1,1024,768]{1,2,0:T(8,128)(2,1)}, u32[]{:S(2)}, u32[]{:S(2)}) collective-permute-start(bf16[1,1024,768]{1,2,0:T(8,128)(2,1)} %get-tuple-element.27), channel_id=1, source_target_pairs={{0,8},{1,9},{2,10},{3,11},{4,12},{5,13},{6,14},{7,15},{8,0},{9,1},... | collective-permute-start | bytes 4718600 | tf_op jit(solution)/shard_map/ppermute | solution.py:8
  254.1 170.8 %collective-permute-start = (bf16[1,1024,768]{1,2,0:T(8,128)(2,1)}, bf16[1,1024,768]{1,2,0:T(8,128)(2,1)}, u32[]{:S(2)}, u32[]{:S(2)}) collective-permute-start(bf16[1,1024,768]{1,2,0:T(8,128)(2,1)} %get-tuple-element.28), channel_id=1, source_target_pairs={{0,8},{1,9},{2,10},{3,11},{4,12},{5,13},{6,14},{7,15},{8,0},{9,1},... | collective-permute-start | bytes 4718600 | tf_op jit(solution)/shard_map/ppermute | solution.py:8
  254.6 203.0 %collective-permute-start.2 = (bf16[1,768,1024]{2,1,0:T(8,128)(2,1)}, bf16[1,768,1024]{2,1,0:T(8,128)(2,1)}, u32[]{:S(2)}, u32[]{:S(2)}) collective-permute-start(bf16[1,768,1024]{2,1,0:T(8,128)(2,1)} %get-tuple-element.26), channel_id=1, source_target_pairs={{0,8},{1,9},{2,10},{3,11},{4,12},{5,13},{6,14},{7,15},{8,0},{9,1},... | collective-permute-start | bytes 4718600 | tf_op jit(solution)/shard_map/ppermute | solution.py:8
  263.4 5.0 %copy-start.4 = (bf16[32,2048]{1,0:T(8,128)(2,1)S(1)}, bf16[32,2048]{1,0:T(8,128)(2,1)}, u32[]{:S(2)}) copy-start(bf16[32,2048]{1,0:T(8,128)(2,1)} %param.15) | copy-start | bytes 393220
  271.1 2.7 copy-start.2
Sparse Core Ops, SparseCore 0:
  131.9 114.9 reduce-scatter.1
where the time goes:
time: 468 us
  waiting for transfers between devices  285 us (61%)
  blocking collectives  43.3 us (9%)
  local copies, waits for them, and re-layouts  33.1 us (7%)
  matrix products  31.7 us (7%)
  other arithmetic  30.4 us (6%)
  starting transfers between devices  29 us (6%)
  between operations  14.9 us (3%)
    ppermute x3, waiting for transfers between devices, from_partner(): lax.ppermute(value, axis, [(i, i ^ 1 << stride) for i in range(lax.axis_s...  172 us
    reduce_scatter x1, waiting for transfers between devices, on_device(): lax.psum_scatter(jnp.concatenate([contract_rows(rows_in, gate_up_grads),...  60.1 us
    all_to_all x1, blocking collectives, on_device(): lax.all_to_all(cot_out, 'expert', split_axis=0, concat_axis=0, tiled=True)  43.3 us
    all_to_all x1, waiting for transfers between devices, on_device(): lax.all_to_all(outbound, 'expert', split_axis=0, concat_axis=0, tiled=True)  27 us
    all_to_all x1, waiting for transfers between devices, on_device(): lax.all_to_all(result, 'expert', split_axis=0, concat_axis=0, tiled=True)  25.9 us
    concatenate x1, other arithmetic, on_device(): jnp.concatenate([contract_rows(rows_in, gate_up_grads), contract_rows(cot...  11.6 us
    dot_general x3, matrix products, contract_cols(): lax.dot_general(left, right, (((1,), (1,)), ((), ())), preferred_element_...  10.9 us
  transfers between devices with their start and end apart: 7, of which 6 were waited for; matrix products, arithmetic and copies ran while one was open for 10% of the time, Pallas kernels for 0%

commit v1 on v0

v1 whole, which is shorter than its diff:
```python
import jax
import jax.numpy as jnp
from jax import lax
from jax.sharding import PartitionSpec as P

F32 = jnp.float32
BF16 = jnp.bfloat16


def dot(left, right, lhs_dim, rhs_dim):
    return lax.dot_general(
        left, right, (((lhs_dim,), (rhs_dim,)), ((), ())), preferred_element_type=F32
    )


def row_picker(column, capacity):
    count = column.shape[0]
    routed = column > 0
    earlier = jnp.arange(count)[:, None] < jnp.arange(count)[None, :]
    position = dot(routed.astype(BF16)[None], earlier.astype(BF16), 1, 0).astype(jnp.int32)
    picks = (position == jnp.arange(capacity, dtype=jnp.int32)[:, None]) & routed[None]
    weight = jnp.sum(jnp.where(picks, column[None], 0.0), axis=1, keepdims=True)
    return picks.astype(BF16), weight


def on_device(tokens, routes, gates, w_gate, w_up, w_down, swap_flags, d_out):
    experts = lax.axis_size("expert")
    groups = lax.axis_size("dp")
    own = lax.axis_index("expert")
    group = lax.axis_index("dp")
    tok_count, width = tokens.shape
    top = routes.shape[1]
    ff = w_gate.shape[2]
    part = width // groups
    rows = experts * tok_count
    capacity = experts * min(
        tok_count, (3 * tok_count * top + 2 * experts - 1) // (2 * experts)
    )
    gate_mat, up_mat, down_mat = w_gate[0], w_up[0], w_down[0]
    swapped = swap_flags[own] == 1
    ids = jnp.arange(experts, dtype=jnp.int32)

    dense = jnp.sum(
        jnp.where(routes[:, :, None] == ids, gates[:, :, None], 0.0), axis=1
    )
    dense_all = lax.all_gather(dense, ("dp", "expert"), tiled=True)
    both = lax.all_gather(
        jnp.concatenate([tokens, d_out], axis=1), "expert", tiled=True
    )

    def column_of(who, expert):
        block = lax.dynamic_slice_in_dim(dense_all, who * rows, rows, 0)
        return jnp.sum(jnp.where(ids == expert, block, 0.0), axis=1)

    picks, weight = row_picker(column_of(group, own), capacity)
    picked = dot(picks, both, 1, 0).astype(BF16)
    x, cot = picked[:, :width], picked[:, width:]

    pre_gate = dot(x, gate_mat, 1, 0)
    pre_up = dot(x, up_mat, 1, 0)
    logistic = jax.nn.sigmoid(pre_gate)
    activated = pre_gate * logistic
    hidden = (activated * pre_up).astype(BF16)
    d_expert = (weight * cot.astype(F32)).astype(BF16)
    d_hidden = dot(d_expert, down_mat, 1, 1)
    d_gate_pre = (
        d_hidden * pre_up * logistic * (1.0 + pre_gate * (1.0 - logistic))
    ).astype(BF16)
    d_up_pre = (d_hidden * activated).astype(BF16)

    half = experts // 2
    trade = [(i, (i + half) % experts) for i in range(experts)]

    def place(mine):
        return jnp.where(swapped, lax.ppermute(mine, "expert", trade), mine)

    acts = (place(hidden), place(jnp.concatenate([d_gate_pre, d_up_pre], axis=1)))

    result = dot(hidden, down_mat, 1, 0).astype(BF16)
    result_f = result.astype(F32)
    mixed = (weight * result_f).astype(BF16)
    mixture = lax.psum_scatter(
        dot(picks, mixed, 0, 0).astype(BF16), "expert", scatter_dimension=0, tiled=True
    )
    d_rows = (dot(d_gate_pre, gate_mat, 1, 1) + dot(d_up_pre, up_mat, 1, 1)).astype(BF16)
    d_tokens = lax.psum_scatter(
        dot(picks, d_rows, 0, 0).astype(BF16), "expert", scatter_dimension=0, tiled=True
    )
    inner = jnp.sum(result_f * cot.astype(F32), axis=1, keepdims=True)
    inner = jnp.sum(picks.astype(F32) * inner, axis=0).reshape(experts, tok_count)
    inner = lax.all_to_all(inner, "expert", split_axis=0, concat_axis=0, tiled=True)
    d_gates = jnp.sum(
        jnp.where(routes[:, :, None] == ids, inner.T[:, None, :], 0.0), axis=2
    )

    placed = jnp.where(swapped, (own + half) % experts, own)
    split = both.reshape(rows, 2, groups, part)
    xs, cots, hiddens, pres = [], [], [], []
    for shift in range(groups):
        target = (group + shift) % groups
        source = (group + groups - shift) % groups
        block = lax.dynamic_index_in_dim(split, target, 2, keepdims=False)
        block = block.reshape(rows, 2 * part)
        h, pre = acts
        if shift:
            ring = [(i, (i + shift) % groups) for i in range(groups)]
            block = lax.ppermute(block, "dp", ring)
            h = lax.ppermute(h, "dp", ring)
            pre = lax.ppermute(pre, "dp", ring)
        choose, scale = row_picker(column_of(source, placed), capacity)
        chosen = dot(choose, block, 1, 0).astype(BF16)
        xs.append(chosen[:, :part])
        cots.append((scale * chosen[:, part:].astype(F32)).astype(BF16))
        hiddens.append(h)
        pres.append(pre)
    g_pre = dot(jnp.concatenate(xs), jnp.concatenate(pres), 0, 0).astype(BF16)
    g_down = dot(jnp.concatenate(hiddens), jnp.concatenate(cots), 0, 0).astype(BF16)
    return (mixture, d_tokens, d_gates, g_pre[None, :, :ff], g_pre[None, :, ff:], g_down[None])


def solution(mesh):
    rows = P(("dp", "expert"), None)
    mats = P("expert", None, None)
    return jax.shard_map(
        on_device,
        mesh=mesh,
        in_specs=(rows, rows, rows, mats, mats, mats, P(), rows),
        out_specs=(rows, rows, rows, P("expert", "dp", None), P("expert", "dp", None), P("expert", None, "dp")),
        check_vma=False,
    )
```

time: 468 us -> 250 us (0.53)
  waiting for transfers between devices: 285 us -> 109 us
  other arithmetic: 30.4 us -> 11 us
  local copies, waits for them, and re-layouts: 33.1 us -> 15.5 us
  starting transfers between devices: 29 us -> 11.7 us
  matrix products: 31.7 us -> 42.8 us
    ppermute x3 -> x5, waiting for transfers between devices: 172 us -> 75.5 us  [the longest x2 54 us: place(): return jnp.where(swapped, lax.ppermute(mine, 'expert', trade), mine)]
    all_to_all x3 -> x1, waiting for transfers between devices: 52.9 us -> 0.24 us  [on_device(): lax.all_to_all(inner, 'expert', split_axis=0, concat_axis=0, tiled=True)]
    all_gather x0 -> x1, blocking collectives: none -> 44.6 us  [on_device(): dense_all = lax.all_gather(dense, ('dp', 'expert'), tiled=True)]
    all_to_all x1 -> x0, blocking collectives: 43.3 us -> none  [on_device(): lax.all_to_all(cot_out, 'expert', split_axis=0, concat_axis=0, tiled=True)]
    reduce_scatter x1 -> x2, waiting for transfers between devices: 60.1 us -> 26.3 us  [the longest x1 26.3 us: on_device(): lax.psum_scatter(dot(picks, d_rows, 0, 0).astype(BF16), 'expert', scatter...]
    all_to_all x3 -> x1, starting transfers between devices: 23.4 us -> 3.49 us  [on_device(): lax.all_to_all(inner, 'expert', split_axis=0, concat_axis=0, tiled=True)]
    gather x4 -> x0, local copies, waits for them, and re-layouts: 19.5 us -> none  [the longest x1 6.45 us: on_device(): cot_pairs[source]]
    dot_general x9 -> x15, matrix products: 31.7 us -> 42.8 us  [dot(): lax.dot_general(left, right, (((lhs_dim,), (rhs_dim,)), ((), ())), prefer...]
  transfers between devices with their start and end apart: 7 -> 9, of which waited for: 6 -> 6; matrix products, arithmetic and copies ran while one was open for 10% -> 21% of each run, Pallas kernels for 0% -> 0%
where the time goes in v1:
time: 250 us; the launch traced here: 249 us
  waiting for transfers between devices  109 us (44%)
  blocking collectives  44.6 us (18%)
  matrix products  42.8 us (17%)
  local copies, waits for them, and re-layouts  15.5 us (6%)
  between operations  14.7 us (6%)
  starting transfers between devices  11.7 us (5%)
  other arithmetic  11 us (4%)
    ppermute x2, waiting for transfers between devices, place(): return jnp.where(swapped, lax.ppermute(mine, 'expert', trade), mine)  54 us
    all_gather x1, blocking collectives, on_device(): dense_all = lax.all_gather(dense, ('dp', 'expert'), tiled=True)  44.6 us
    dot_general x15, matrix products, dot(): lax.dot_general(left, right, (((lhs_dim,), (rhs_dim,)), ((), ())), prefer...  42.8 us
    reduce_scatter x1, waiting for transfers between devices, on_device(): lax.psum_scatter(dot(picks, d_rows, 0, 0).astype(BF16), 'expert', scatter...  26.3 us
    ppermute x1, waiting for transfers between devices, on_device(): h = lax.ppermute(h, 'dp', ring)  21.4 us
    all_gather x1, waiting for transfers between devices, on_device(): lax.all_gather(jnp.concatenate([tokens, d_out], axis=1), 'expert', tiled=...  7.01 us
    all_gather x1, local copies, waits for them, and re-layouts, on_device(): lax.all_gather(jnp.concatenate([tokens, d_out], axis=1), 'expert', tiled=...  6.58 us
  transfers between devices with their start and end apart: 9, of which 6 were waited for; matrix products, arithmetic and copies ran while one was open for 21% of the time, Pallas kernels for 0%

profile of v1, /device:TPU:0, one launch (start us, length us, event | category | flops | bytes accessed | tf_op | source)
XLA Modules:
  0.0 249.3 jit_solution(8894204136714402894)
XLA Ops:
  7.2 0.0 copy-start
  7.2 0.0 all-gather.3.cloned.1.call-start
  7.2 1.8 pad_maximum_fusion.1
  9.1 0.0 all-gather.3.cloned.1.call-update
  9.1 0.0 reduce-scatter.3.cloned.1.call-start
  9.2 0.7 select_reduce_fusion.4
  9.9 44.6 %all-gather = f32[32,32,16]{1,2,0:T(8,128)S(1)} all-gather(f32[1,32,16]{1,2,0:T(8,128)S(1)} %bitcast.58), channel_id=1, replica_groups=mesh['dp'=2,'expert'=16] {'dp','expert'}, dimensions={0}, use_global_device_ids=true | all-gather | bytes 67584 | tf_op jit(solution)/shard_map/all_gather | solution.py:46
  54.5 0.1 copy.35
  54.6 0.1 reshape.64
  54.8 1.2 dynamic_slice.20
  56.7 0.1 select_reduce_fusion.6
  56.8 0.2 fusion.47
  57.0 7.0 %all-gather.3.cloned.1.call-done = bf16[512,4096]{1,0:T(8,128)(2,1)} async-done(((bf16[32,4096]{1,0:T(8,128)(2,1)}), bf16[512,4096]{1,0:T(8,128)(2,1)}) %all-gather.3.cloned.1.call-update) | async-done | bytes 4194320 | tf_op jit(solution)/shard_map/all_gather | solution.py:47
  64.0 4.1 %convolution_convert_fusion = bf16[384,4096]{1,0:T(8,128)(2,1)S(1)} fusion(bf16[512,4096]{1,0:T(8,128)(2,1)} %all-gather.3.cloned.1.call-done, s32[512]{0:T(512)S(1)} %convert_element_type.87, pred[512]{0:T(512)(128)(4,1)S(1)} %broadcast_compare_fusion.2), kind=kOutput, calls=%fused_computation | convolution fusion | flops 1612578816 | bytes 7342592 | tf_op jit(solution)/shard_map/dot_general | solution.py:11
  68.2 0.0 copy-done.11
  68.2 0.0 copy-start.10
  68.2 1.4 fusion.13
  69.6 1.6 copy-done.10
  71.2 2.4 multiply_convert_fusion.4
  73.7 1.6 fusion.2
  75.2 0.3 multiply_reduce_fusion
  75.5 2.8 %convolution_convert_fusion.3 = bf16[512,2048]{1,0:T(8,128)(2,1)} fusion(bf16[384,2048]{1,0:T(8,128)(2,1)S(1)} %get-tuple-element.20, f32[384]{0:T(512)S(1)} %get-tuple-element.10, s32[512]{0:T(512)S(1)} %convert_element_type.87, pred[512]{0:T(512)(128)(4,1)S(1)} %broadcast_compare_fusion.2), kind=kOutput, calls=%fused_computation.22 | convolution fusion | flops 809107456 | bytes 3674112 | tf_op jit(solution)/shard_map/dot_general | solution.py:11
  78.3 0.0 reduce-scatter.3.cloned.1.call-update
  78.3 0.2 reduce-scatter.5.cloned.1.call-start
  78.6 0.2 fusion.45
  78.8 0.2 fusion.46
  79.0 3.8 %multiply_convert_fusion.3 = (bf16[384,768]{1,0:T(8,128)(2,1)S(1)}, bf16[384,768]{1,0:T(8,128)(2,1)S(1)}) fusion(f32[384,768]{1,0:T(8,128)} %copy-done.13, f32[384,768]{1,0:T(8,128)} %get-tuple-element.18, bf16[1,768,2048]{2,1,0:T(8,128)(2,1)S(1)} %copy-done, f32[384]{0:T(512)S(1)} %get-tuple-element.10, bf16[384,4096]{1,0:T(8,128)(2,1)} %copy-done.12), kind=kOutput, calls=%fused_computation.51 | convolution fusion | flops 1214152704 | bytes 8259072 | tf_op jit(solution)/shard_map/dot_general | solution.py:11
  82.8 0.0 copy-start.4
  82.8 0.8 copy-done.2
  83.6 1.1 pad_maximum_fusion
  84.7 2.3 collective-permute-start.1
  87.0 6.6 %copy.37 = bf16[512,4096]{0,1:T(8,128)(2,1)} copy(bf16[512,4096]{1,0:T(8,128)(2,1)} %all-gather.3.cloned.1.call-done) | data formatting | bytes 8388608 | tf_op jit(solution)/shard_map/all_gather | solution.py:47
  93.5 5.4 %fusion.7 = f32[384,2048]{1,0:T(8,128)} fusion(bf16[384,768]{1,0:T(8,128)(2,1)} %copy-done.4, bf16[1,2048,768]{2,1,0:T(8,128)(2,1)} %param.12), kind=kOutput, calls=%fused_computation.12 | convolution fusion | flops 1207959552 | bytes 6881280 | tf_op jit(solution)/shard_map/dot_general | solution.py:11
  98.9 2.3 constant_dynamic-slice_fusion.1
  101.2 1.5 collective-permute-start
  102.8 7.1 %convolution_convert_fusion.2 = bf16[512,2048]{1,0:T(8,128)(2,1)} fusion(f32[384,2048]{1,0:T(8,128)} %fusion.7, bf16[384,768]{1,0:T(8,128)(2,1)} %copy-done.2, bf16[1,2048,768]{2,1,0:T(8,128)(2,1)} %param.11, s32[512]{0:T(512)S(1)} %convert_element_type.87, pred[512]{0:T(512)(128)(4,1)S(1)} %broadcast_compare_fusion.2), kind=kOutput, calls=%fused_computation.21 | convolution fusion | flops 2016280576 | bytes 8980992 | tf_op jit(solution)/shard_map/dot_general | solution.py:11
  109.9 0.0 reduce-scatter.5.cloned.1.call-update
  109.9 0.4 select_reduce_fusion
  110.3 0.6 collective-permute-start.3
  111.0 2.7 %convolution_convert_fusion.5 = bf16[384,2048]{1,0:T(8,128)(2,1)S(1)} fusion(bf16[512,2048]{0,1:T(8,128)(2,1)} %bitcast.57, s32[512]{0:T(512)S(1)} %convert_element_type.102, pred[512]{0:T(512)(128)(4,1)S(1)} %broadcast_compare_fusion.1), kind=kOutput, calls=%fused_computation.25 | convolution fusion | flops 806486016 | bytes 3672576 | tf_op jit(solution)/shard_map/dot_general | solution.py:11
  113.7 0.0 copy-start.6
  113.7 51.6 %collective-permute-done.1 = bf16[384,1536]{1,0:T(8,128)(2,1)} collective-permute-done((bf16[384,1536]{1,0:T(8,128)(2,1)}, bf16[384,1536]{1,0:T(8,128)(2,1)}, u32[]{:S(2)}, u32[]{:S(2)}) %collective-permute-start.1) | collective-permute-done | bytes 1179680 | tf_op jit(solution)/shard_map/ppermute | solution.py:75
  165.3 2.6 %broadcast_select_fusion = bf16[384,1536]{1,0:T(8,128)(2,1)} fusion(bf16[384,1536]{1,0:T(8,128)(2,1)} %collective-permute-done.1, pred[]{:T(512)} %bitcast.8, bf16[384,768]{1,0:T(8,128)(2,1)S(1)} %copy-done.5, bf16[384,768]{1,0:T(8,128)(2,1)S(1)} %copy-done.3), kind=kLoop, calls=%fused_computation.55 | loop fusion | flops 2949120 | bytes 3538945 | tf_op jit(solution)/shard_map/jit(_where)/select_n | solution.py:75
  167.9 1.7 collective-permute-start.2
  169.6 1.1 multiply_convert_fusion.1
  170.7 0.7 all_to_all.8
  171.3 3.5 %all-to-all-start = ((f32[16,1,32]{2,1,0:T(1,128)}), f32[16,1,32]{2,1,0:T(1,128)S(1)}, u32[]{:S(2)}, u32[]{:S(2)}) async-start(f32[16,1,32]{2,1,0:T(1,128)} %bitcast.5), calls=%async_computation.2 | async-start | bytes 16384 | tf_op jit(solution)/shard_map/all_to_all | solution.py:91
  174.8 2.4 collective-permute-done.3
  177.2 2.0 broadcast_select_fusion.1
  179.2 1.7 collective-permute-start.4
  181.0 0.2 all-to-all-done
  181.2 0.6 select_reduce_fusion.3
  181.8 0.0 collective-permute-done
  181.8 2.6 %convolution_convert_fusion.4 = bf16[384,2048]{1,0:T(8,128)(2,1)S(1)} fusion(bf16[512,2048]{0,1:T(8,128)(2,1)} %collective-permute-done, s32[512]{0:T(512)S(1)} %convert_element_type.104, pred[512]{0:T(512)(128)(4,1)S(1)} %broadcast_compare_fusion), kind=kOutput, calls=%fused_computation.24 | convolution fusion | flops 806486016 | bytes 3672576 | tf_op jit(solution)/shard_map/dot_general | solution.py:11
  184.4 0.0 copy-start.7
  184.4 0.1 slice.35
  184.5 0.2 multiply_convert_fusion
  184.7 0.0 slice-start
  184.7 21.4 %collective-permute-done.4 = bf16[384,768]{1,0:T(8,128)(2,1)} collective-permute-done((bf16[384,768]{1,0:T(8,128)(2,1)}, bf16[384,768]{1,0:T(8,128)(2,1)}, u32[]{:S(2)}, u32[]{:S(2)}) %collective-permute-start.4) | collective-permute-done | bytes 589856 | tf_op jit(solution)/shard_map/ppermute | solution.py:108
  206.2 3.8 %fusion.33 = bf16[1,768,1024]{2,1,0:T(8,128)(2,1)} fusion(bf16[384,1024]{1,0:T(8,128)(2,1)S(1)} %multiply_convert_fusion, bf16[384,1024]{1,0:T(8,128)(2,1)S(1)} %copy-done.7, bf16[384,768]{1,0:T(8,128)(2,1)} %collective-permute-done.4, bf16[384,768]{1,0:T(8,128)(2,1)} %broadcast_select_fusion.1), kind=kOutput, calls=%fused_computation.42 | convolution fusion | flops 1214251008 | bytes 4325376 | tf_op jit(solution)/shard_map/dot_general | solution.py:11
  210.0 0.0 collective-permute-done.2
  210.0 4.6 %convolution_convert_fusion.1 = bf16[1024,1536]{1,0:T(8,128)(2,1)S(1)} fusion(bf16[384,1536]{1,0:T(8,128)(2,1)} %collective-permute-done.2, bf16[384,1536]{1,0:T(8,128)(2,1)} %broadcast_select_fusion, bf16[384,1024]{1,0:T(8,128)(2,1)S(1)} %slice.35, bf16[384,1024]{1,0:T(8,128)(2,1)S(1)} %slice-done), kind=kOutput, calls=%fused_computation.4 | convolution fusion | flops 2425356288 | bytes 7077888 | tf_op jit(solution)/shard_map/dot_general | solution.py:11
  214.6 1.9 slice_bitcast_fusion
  216.5 26.3 %reduce-scatter.5.cloned.1.call-done = bf16[32,2048]{1,0:T(8,128)(2,1)} async-done(((bf16[512,2048]{1,0:T(8,128)(2,1)}), bf16[32,2048]{1,0:T(8,128)(2,1)}) %reduce-scatter.5.cloned.1.call-update) | async-done | bytes 131088 | tf_op jit(solution)/shard_map/reduce_scatter | solution.py:86
  (33 shorter events, 0.1 us)
Async XLA Ops:
  7.2 66.5 %copy-start = (bf16[1,768,2048]{2,1,0:T(8,128)(2,1)S(1)}, bf16[1,768,2048]{2,1,0:T(8,128)(2,1)}, u32[]{:S(2)}) copy-start(bf16[1,768,2048]{2,1,0:T(8,128)(2,1)} %param.13) | copy-start | bytes 9437188
  7.2 56.8 %all-gather.3.cloned.1.call-start = ((), (), s32[]{:S(2)}) async-start(), calls=%async_computation.3 | async-start | bytes 4456448 | tf_op jit(solution)/shard_map/all_gather | solution.py:47
  9.1 207.4 %reduce-scatter.3.cloned.1.call-start = ((), (), s32[]{:S(2)}) async-start(), calls=%async_computation.4 | async-start | bytes 2228224 | tf_op jit(solution)/shard_map/reduce_scatter | solution.py:82
  64.0 4.1 %copy-start.11 = (bf16[1,2048,768]{2,1,0:T(8,128)(2,1)S(1)}, bf16[1,2048,768]{2,1,0:T(8,128)(2,1)}, u32[]{:S(2)}) copy-start(bf16[1,2048,768]{2,1,0:T(8,128)(2,1)} %param.11) | copy-start | bytes 9437188
  68.2 5.5 %copy-start.12 = (bf16[384,4096]{1,0:T(8,128)(2,1)}, bf16[384,4096]{1,0:T(8,128)(2,1)S(1)}, u32[]{:S(2)}) copy-start(bf16[384,4096]{1,0:T(8,128)(2,1)S(1)} %convolution_convert_fusion) | copy-start | bytes 9437188
  68.2 3.0 %copy-start.10 = (bf16[1,2048,768]{2,1,0:T(8,128)(2,1)S(1)}, bf16[1,2048,768]{2,1,0:T(8,128)(2,1)}, u32[]{:S(2)}) copy-start(bf16[1,2048,768]{2,1,0:T(8,128)(2,1)} %param.12) | copy-start | bytes 9437188
  71.2 2.4 copy-start.13
  73.6 1.6 copy-start.8
  78.3 164.4 %reduce-scatter.5.cloned.1.call-start = ((), (), s32[]{:S(2)}) async-start(), calls=%async_computation.5 | async-start | bytes 2228224 | tf_op jit(solution)/shard_map/reduce_scatter | solution.py:86
  82.8 0.8 copy-start.2
  82.8 1.9 copy-start.4
  84.7 80.6 %collective-permute-start.1 = (bf16[384,1536]{1,0:T(8,128)(2,1)}, bf16[384,1536]{1,0:T(8,128)(2,1)}, u32[]{:S(2)}, u32[]{:S(2)}) collective-permute-start(bf16[384,1536]{1,0:T(8,128)(2,1)} %pad_maximum_fusion), channel_id=1, source_target_pairs={{0,8},{1,9},{2,10},{3,11},{4,12},{5,13},{6,14},{7,15},{8,0},{9,1},... | collective-permute-start | bytes 3538952 | tf_op jit(solution)/shard_map/ppermute | solution.py:75
  93.5 5.4 %copy-start.1 = (bf16[512,4096]{0,1:T(8,128)(2,1)S(1)}, bf16[512,4096]{0,1:T(8,128)(2,1)}, u32[]{:S(2)}) copy-start(bf16[512,4096]{0,1:T(8,128)(2,1)} %copy.37) | copy-start | bytes 12582916
  101.2 80.6 %collective-permute-start = (bf16[512,2048]{0,1:T(8,128)(2,1)}, bf16[512,2048]{0,1:T(8,128)(2,1)}, u32[]{:S(2)}, u32[]{:S(2)}) collective-permute-start(bf16[512,2048]{0,1:T(8,128)(2,1)} %bitcast.13), channel_id=1, source_target_pairs={{0,16},{16,0},{1,17},{17,1},{2,18},{18,2},{3,19},{19,3},{4,20},{20... | collective-permute-start | bytes 6291464 | tf_op jit(solution)/shard_map/ppermute | solution.py:107
  110.3 66.9 %collective-permute-start.3 = (bf16[384,768]{1,0:T(8,128)(2,1)}, bf16[384,768]{1,0:T(8,128)(2,1)}, u32[]{:S(2)}, u32[]{:S(2)}) collective-permute-start(bf16[384,768]{1,0:T(8,128)(2,1)} %copy-done.8), channel_id=1, source_target_pairs={{0,8},{1,9},{2,10},{3,11},{4,12},{5,13},{6,14},{7,15},{8,0},{9,1},... | collective-permute-start | bytes 1769480 | tf_op jit(solution)/shard_map/ppermute | solution.py:75
  111.0 54.3 %copy-start.3 = (bf16[384,768]{1,0:T(8,128)(2,1)S(1)}, bf16[384,768]{1,0:T(8,128)(2,1)}, u32[]{:S(2)}) copy-start(bf16[384,768]{1,0:T(8,128)(2,1)} %copy-done.2) | copy-start | bytes 1769476
  111.0 54.3 %copy-start.5 = (bf16[384,768]{1,0:T(8,128)(2,1)S(1)}, bf16[384,768]{1,0:T(8,128)(2,1)}, u32[]{:S(2)}) copy-start(bf16[384,768]{1,0:T(8,128)(2,1)} %copy-done.4) | copy-start | bytes 1769476
  113.7 57.0 %copy-start.6 = (bf16[384,2048]{1,0:T(8,128)(2,1)}, bf16[384,2048]{1,0:T(8,128)(2,1)S(1)}, u32[]{:S(2)}) copy-start(bf16[384,2048]{1,0:T(8,128)(2,1)S(1)} %convolution_convert_fusion.5) | copy-start | bytes 4718596
  167.9 42.2 %collective-permute-start.2 = (bf16[384,1536]{1,0:T(8,128)(2,1)}, bf16[384,1536]{1,0:T(8,128)(2,1)}, u32[]{:S(2)}, u32[]{:S(2)}) collective-permute-start(bf16[384,1536]{1,0:T(8,128)(2,1)} %broadcast_select_fusion), channel_id=1, source_target_pairs={{0,16},{16,0},{1,17},{17,1},{2,18},{18,2},{3,19},{19,3},{4,20},{20... | collective-permute-start | bytes 3538952 | tf_op jit(solution)/shard_map/ppermute | solution.py:109
  169.6 11.6 %copy-start.9 = (s32[32,8]{0,1:T(8,128)S(1)}, s32[32,8]{0,1:T(8,128)}, u32[]{:S(2)}) copy-start(s32[32,8]{0,1:T(8,128)} %param.9) | copy-start | bytes 3076
  171.3 9.9 %all-to-all-start = ((f32[16,1,32]{2,1,0:T(1,128)}), f32[16,1,32]{2,1,0:T(1,128)S(1)}, u32[]{:S(2)}, u32[]{:S(2)}) async-start(f32[16,1,32]{2,1,0:T(1,128)} %bitcast.5), calls=%async_computation.2 | async-start | bytes 16384 | tf_op jit(solution)/shard_map/all_to_all | solution.py:91
  179.2 27.0 %collective-permute-start.4 = (bf16[384,768]{1,0:T(8,128)(2,1)}, bf16[384,768]{1,0:T(8,128)(2,1)}, u32[]{:S(2)}, u32[]{:S(2)}) collective-permute-start(bf16[384,768]{1,0:T(8,128)(2,1)} %broadcast_select_fusion.1), channel_id=1, source_target_pairs={{0,16},{16,0},{1,17},{17,1},{2,18},{18,2},{3,19},{19,3},{4,20},{20... | collective-permute-start | bytes 1769480 | tf_op jit(solution)/shard_map/ppermute | solution.py:108
  184.4 21.8 %copy-start.7 = (bf16[384,1024]{1,0:T(8,128)(2,1)S(1)}, bf16[384,1024]{1,0:T(8,128)(2,1)}, u32[]{:S(2)}) copy-start(bf16[384,1024]{1,0:T(8,128)(2,1)} %multiply_convert_fusion.1) | copy-start | bytes 2359300
  184.7 25.3 %slice-start = ((bf16[384,2048]{1,0:T(8,128)(2,1)}), bf16[384,1024]{1,0:T(8,128)(2,1)S(1)}, s32[]{:S(2)}) async-start(bf16[384,2048]{1,0:T(8,128)(2,1)} %copy-done.6), calls=%async_computation.6 | async-start | bytes 1572864 | tf_op jit(solution)/shard_map/slice | solution.py:112
Sparse Core Ops, SparseCore 0:
  10.7 53.2 all-gather.2
  78.5 83.5 reduce-scatter.2
  166.8 75.9 reduce-scatter.4

commit v2 on v1

--- a/solution.py
+++ b/solution.py
@@ -23,6 +23,54 @@
     return picks.astype(BF16), weight
 
 
+def bit_of(index, bit):
+    return (index // (1 << bit)) % 2
+
+
+def swap_bit(value, bit):
+    size = lax.axis_size("expert")
+    return lax.ppermute(value, "expert", [(i, i ^ (1 << bit)) for i in range(size)])
+
+
+def gather_rows(block, order):
+    own = lax.axis_index("expert")
+    held, done = block, []
+    for bit in order:
+        other = swap_bit(held, bit)
+        at = sum(b > bit for b in done)
+        high = bit_of(own, bit) == 1
+        held = jnp.stack(
+            [jnp.where(high, other, held), jnp.where(high, held, other)], axis=at
+        )
+        done.append(bit)
+    return held.reshape(-1, block.shape[-1])
+
+
+def scatter_sum(partial, bits):
+    own = lax.axis_index("expert")
+    size, width = partial.shape[0] >> bits, partial.shape[1]
+    for bit in range(bits):
+        pairs = partial.reshape(-1, 2, size, width)
+        high = bit_of(own, bit) == 1
+        keep = jnp.where(high, pairs[:, 1], pairs[:, 0])
+        give = jnp.where(high, pairs[:, 0], pairs[:, 1])
+        partial = (keep.astype(F32) + swap_bit(give, bit).astype(F32)).astype(BF16)
+    return partial.reshape(size, width)
+
+
+def after(value, *others):
+    return lax.optimization_barrier((value, *others))[0]
+
+
+def terms_of(value):
+    terms = []
+    for _ in range(3):
+        term = lax.reduce_precision(value, 8, 7)
+        terms.append(term.astype(BF16))
+        value = value - term
+    return terms
+
+
 def on_device(tokens, routes, gates, w_gate, w_up, w_down, swap_flags, d_out):
     experts = lax.axis_size("expert")
     groups = lax.axis_size("dp")
@@ -43,18 +91,22 @@
     dense = jnp.sum(
         jnp.where(routes[:, :, None] == ids, gates[:, :, None], 0.0), axis=1
     )
-    dense_all = lax.all_gather(dense, ("dp", "expert"), tiled=True)
-    both = lax.all_gather(
-        jnp.concatenate([tokens, d_out], axis=1), "expert", tiled=True
+    bits = experts.bit_length() - 1
+    spare = jnp.zeros((tok_count, -3 * experts % 128), BF16)
+    first = gather_rows(
+        jnp.concatenate([tokens, *terms_of(dense), spare], axis=1), range(bits - 1, -1, -1)
     )
+    d_out_all = gather_rows(d_out, [*range(1, bits), 0])
+    tokens_all, table = first[:, :width], first[:, width:]
 
-    def column_of(who, expert):
-        block = lax.dynamic_slice_in_dim(dense_all, who * rows, rows, 0)
+    def column_of(table, expert):
+        terms = table[:, : 3 * experts].astype(F32).reshape(rows, 3, experts)
+        block = terms[:, 0] + (terms[:, 1] + terms[:, 2])
         return jnp.sum(jnp.where(ids == expert, block, 0.0), axis=1)
 
-    picks, weight = row_picker(column_of(group, own), capacity)
-    picked = dot(picks, both, 1, 0).astype(BF16)
-    x, cot = picked[:, :width], picked[:, width:]
+    picks, weight = row_picker(column_of(table, own), capacity)
+    x = dot(picks, tokens_all, 1, 0).astype(BF16)
+    cot = dot(picks, d_out_all, 1, 0).astype(BF16)
 
     pre_gate = dot(x, gate_mat, 1, 0)
     pre_up = dot(x, up_mat, 1, 0)
@@ -71,21 +123,16 @@
     half = experts // 2
     trade = [(i, (i + half) % experts) for i in range(experts)]
 
-    def place(mine):
-        return jnp.where(swapped, lax.ppermute(mine, "expert", trade), mine)
-
-    acts = (place(hidden), place(jnp.concatenate([d_gate_pre, d_up_pre], axis=1)))
+    pres = jnp.concatenate([d_gate_pre, d_up_pre], axis=1)
+    far_hidden = lax.ppermute(hidden, "expert", trade)
+    far_pres = lax.ppermute(pres, "expert", trade)
 
     result = dot(hidden, down_mat, 1, 0).astype(BF16)
     result_f = result.astype(F32)
     mixed = (weight * result_f).astype(BF16)
-    mixture = lax.psum_scatter(
-        dot(picks, mixed, 0, 0).astype(BF16), "expert", scatter_dimension=0, tiled=True
-    )
+    mixture = scatter_sum(dot(picks, mixed, 0, 0).astype(BF16), bits)
     d_rows = (dot(d_gate_pre, gate_mat, 1, 1) + dot(d_up_pre, up_mat, 1, 1)).astype(BF16)
-    d_tokens = lax.psum_scatter(
-        dot(picks, d_rows, 0, 0).astype(BF16), "expert", scatter_dimension=0, tiled=True
-    )
+    d_tokens = scatter_sum(dot(picks, d_rows, 0, 0).astype(BF16), bits)
     inner = jnp.sum(result_f * cot.astype(F32), axis=1, keepdims=True)
     inner = jnp.sum(picks.astype(F32) * inner, axis=0).reshape(experts, tok_count)
     inner = lax.all_to_all(inner, "expert", split_axis=0, concat_axis=0, tiled=True)
@@ -94,26 +141,31 @@
     )
 
     placed = jnp.where(swapped, (own + half) % experts, own)
-    split = both.reshape(rows, 2, groups, part)
-    xs, cots, hiddens, pres = [], [], [], []
+    acts = (
+        jnp.where(swapped, after(far_hidden, mixture), hidden),
+        jnp.where(swapped, after(far_pres, d_tokens), pres),
+    )
+    xs, cots, hiddens, pre_parts = [], [], [], []
     for shift in range(groups):
         target = (group + shift) % groups
-        source = (group + groups - shift) % groups
-        block = lax.dynamic_index_in_dim(split, target, 2, keepdims=False)
-        block = block.reshape(rows, 2 * part)
+        block = jnp.concatenate(
+            [lax.dynamic_slice_in_dim(a, target * part, part, 1) for a in (tokens_all, d_out_all)]
+            + [table],
+            axis=1,
+        )
         h, pre = acts
         if shift:
             ring = [(i, (i + shift) % groups) for i in range(groups)]
             block = lax.ppermute(block, "dp", ring)
             h = lax.ppermute(h, "dp", ring)
             pre = lax.ppermute(pre, "dp", ring)
-        choose, scale = row_picker(column_of(source, placed), capacity)
-        chosen = dot(choose, block, 1, 0).astype(BF16)
+        choose, scale = row_picker(column_of(block[:, 2 * part :], placed), capacity)
+        chosen = dot(choose, block[:, : 2 * part], 1, 0).astype(BF16)
         xs.append(chosen[:, :part])
         cots.append((scale * chosen[:, part:].astype(F32)).astype(BF16))
         hiddens.append(h)
-        pres.append(pre)
-    g_pre = dot(jnp.concatenate(xs), jnp.concatenate(pres), 0, 0).astype(BF16)
+        pre_parts.append(pre)
+    g_pre = dot(jnp.concatenate(xs), jnp.concatenate(pre_parts), 0, 0).astype(BF16)
     g_down = dot(jnp.concatenate(hiddens), jnp.concatenate(cots), 0, 0).astype(BF16)
     return (mixture, d_tokens, d_gates, g_pre[None, :, :ff], g_pre[None, :, ff:], g_down[None])
 

time: 250 us -> 275 us (1.10)
  blocking collectives: 44.6 us -> 0 us
  waiting for transfers between devices: 109 us -> 152 us
  starting transfers between devices: 11.7 us -> 31.8 us
  local copies, waits for them, and re-layouts: 15.5 us -> 28.6 us
  between operations: 14.7 us -> 1.99 us
  other arithmetic: 11 us -> 22.4 us
  matrix products: 42.8 us -> 37.9 us
    all_gather x1 -> x0, blocking collectives: 44.6 us -> none  [on_device(): dense_all = lax.all_gather(dense, ('dp', 'expert'), tiled=True)]
    ppermute x1, waiting for transfers between devices: 0.01 us -> 42.4 us  [on_device(): block = lax.ppermute(block, 'dp', ring)]
    ppermute x2 -> x18, waiting for transfers between devices: 54 us -> 81.6 us  [the longest x16 81.6 us: swap_bit(): lax.ppermute(value, 'expert', [(i, i ^ 1 << bit) for i in range(size)])]
    reduce_scatter x2 -> x0, waiting for transfers between devices: 26.3 us -> none  [the longest x1 26.3 us: on_device(): lax.psum_scatter(dot(picks, d_rows, 0, 0).astype(BF16), 'expert', scatter...]
    ppermute x2 -> x18, starting transfers between devices: 2.89 us -> 20.1 us  [the longest x16 17.4 us: swap_bit(): lax.ppermute(value, 'expert', [(i, i ^ 1 << bit) for i in range(size)])]
    unnamed x29 -> x75, local copies, waits for them, and re-layouts: 2.63 us -> 18.1 us
    another operation x0 -> x16, other arithmetic: none -> 8.57 us  [gather_rows(): jnp.stack([jnp.where(high, other, held), jnp.where(high, held, other)], a...]
    all_gather x1 -> x0, waiting for transfers between devices: 7.01 us -> none  [on_device(): lax.all_gather(jnp.concatenate([tokens, d_out], axis=1), 'expert', tiled=...]
  transfers between devices with their start and end apart: 9 -> 22, of which waited for: 6 -> 12; matrix products, arithmetic and copies ran while one was open for 21% -> 19% of each run, Pallas kernels for 0% -> 0%
where the time goes in v2:
time: 275 us
  waiting for transfers between devices  152 us (55%)
  matrix products  37.9 us (14%)
  starting transfers between devices  31.8 us (12%)
  local copies, waits for them, and re-layouts  28.6 us (10%)
  other arithmetic  22.4 us (8%)
    ppermute x16, waiting for transfers between devices, swap_bit(): lax.ppermute(value, 'expert', [(i, i ^ 1 << bit) for i in range(size)])  81.6 us
    ppermute x1, waiting for transfers between devices, on_device(): block = lax.ppermute(block, 'dp', ring)  42.4 us
    dot_general x16, matrix products, dot(): lax.dot_general(left, right, (((lhs_dim,), (rhs_dim,)), ((), ())), prefer...  37.9 us
    ppermute x1, waiting for transfers between devices, on_device(): h = lax.ppermute(h, 'dp', ring)  28 us
    unnamed x75, local copies, waits for them, and re-layouts  18.1 us
    ppermute x16, starting transfers between devices, swap_bit(): lax.ppermute(value, 'expert', [(i, i ^ 1 << bit) for i in range(size)])  17.4 us
    another operation x16, other arithmetic, gather_rows(): jnp.stack([jnp.where(high, other, held), jnp.where(high, held, other)], a...  8.57 us
    all_to_all x1, starting transfers between devices, on_device(): lax.all_to_all(inner, 'expert', split_axis=0, concat_axis=0, tiled=True)  7.03 us
  transfers between devices with their start and end apart: 22, of which 12 were waited for; matrix products, arithmetic and copies ran while one was open for 19% of the time, Pallas kernels for 0%

profile of v2, /device:TPU:0, one launch (start us, length us, event | category | flops | bytes accessed | tf_op | source)
XLA Modules:
  0.0 274.6 jit_solution(8775963335973400596)
XLA Ops:
  0.6 3.0 %collective-permute-start.8 = (bf16[32,2048]{1,0:T(8,128)(2,1)}, bf16[32,2048]{1,0:T(8,128)(2,1)S(1)}, u32[]{:S(2)}, u32[]{:S(2)}) collective-permute-start(bf16[32,2048]{1,0:T(8,128)(2,1)} %param.15), channel_id=1, source_target_pairs={{0,2},{1,3},{2,0},{3,1},{4,6},{5,7},{6,4},{7,5},{8,10},{9,11},{10,... | collective-permute-start | bytes 393224 | tf_op jit(solution)/shard_map/ppermute | solution.py:32
  3.7 0.7 select_reduce_fusion.4
  4.7 1.0 concatenate.24
  5.7 2.6 collective-permute-start
  8.3 0.9 select_bitcast_fusion.20
  9.3 1.6 collective-permute-start.9
  10.9 3.9 %collective-permute-done = bf16[32,2176]{1,0:T(8,128)(2,1)S(1)} collective-permute-done((bf16[32,2176]{1,0:T(8,128)(2,1)S(1)}, bf16[32,2176]{1,0:T(8,128)(2,1)S(1)}, u32[]{:S(2)}, u32[]{:S(2)}) %collective-permute-start) | collective-permute-done | bytes 139296 | tf_op jit(solution)/shard_map/ppermute | solution.py:32
  15.6 4.6 %collective-permute-done.9 = bf16[2,32,2048]{2,1,0:T(8,128)(2,1)S(1)} collective-permute-done((bf16[2,32,2048]{2,1,0:T(8,128)(2,1)S(1)}, bf16[2,32,2048]{2,1,0:T(8,128)(2,1)S(1)}, u32[]{:S(2)}, u32[]{:S(2)}) %collective-permute-start.9) | collective-permute-done | bytes 262176 | tf_op jit(solution)/shard_map/ppermute | solution.py:32
  20.3 1.5 collective-permute-start.10
  21.8 7.2 %collective-permute-done.1 = bf16[2,32,2176]{2,1,0:T(8,128)(2,1)S(1)} collective-permute-done((bf16[2,32,2176]{2,1,0:T(8,128)(2,1)S(1)}, bf16[2,32,2176]{2,1,0:T(8,128)(2,1)S(1)}, u32[]{:S(2)}, u32[]{:S(2)}) %collective-permute-start.1) | collective-permute-done | bytes 278560 | tf_op jit(solution)/shard_map/ppermute | solution.py:32
  29.4 14.1 %collective-permute-done.10 = bf16[2,2,32,2048]{3,2,1,0:T(8,128)(2,1)S(1)} collective-permute-done((bf16[2,2,32,2048]{3,2,1,0:T(8,128)(2,1)S(1)}, bf16[2,2,32,2048]{3,2,1,0:T(8,128)(2,1)S(1)}, u32[]{:S(2)}, u32[]{:S(2)}) %collective-permute-start.10) | collective-permute-done | bytes 524320 | tf_op jit(solution)/shard_map/ppermute | solution.py:32
  43.6 1.2 pad_maximum_fusion.5
  45.0 0.8 copy-done.8
  45.7 1.1 pad_maximum_fusion.4
  47.8 1.7 select_bitcast_fusion.4
  49.5 1.5 pad_maximum_fusion.2
  51.0 1.5 select_bitcast_fusion.1
  52.7 1.4 copy-done.2
  54.1 1.6 slice.159
  55.9 4.3 %constant_dynamic-slice_fusion.2 = (bf16[512,1024]{1,0:T(8,128)(2,1)}, bf16[512,1024]{1,0:T(8,128)(2,1)}, bf16[512,1024]{1,0:T(8,128)(2,1)}, bf16[512,1024]{1,0:T(8,128)(2,1)}) fusion(bf16[512,2048]{1,0:T(8,128)(2,1)} %bitcast.248, s32[]{:T(128)S(6)} %select_n.442, s32[]{:T(128)S(6)} %select_n.444, bf16[512,2048]{1,0:T(8,128)(2,1)} %slice.159), kind=kLoop, calls=%fused_computation.177 | loop fusion | bytes 8388616 | tf_op jit(solution)/shard_map/dynamic_slice | solution.py:152
  60.1 2.3 copy.168
  62.4 2.3 copy.171
  64.7 3.1 %pad_maximum_fusion.1 = bf16[512,2176]{0,1:T(8,128)(2,1)} fusion(bf16[512,128]{0,1:T(8,128)(2,1)S(1)} %copy.169, bf16[512,1024]{0,1:T(8,128)(2,1)} %copy.168, bf16[512,1024]{0,1:T(8,128)(2,1)} %copy.171), kind=kLoop, calls=%fused_computation.31 | loop fusion | flops 6684672 | bytes 4456448 | tf_op jit(solution)/shard_map/concatenate | solution.py:151
  67.8 1.5 collective-permute-start.16
  70.5 0.9 slice.155
  71.6 2.3 copy.167
  73.9 2.3 copy.170
  76.2 42.4 %collective-permute-done.16 = bf16[512,2176]{0,1:T(8,128)(2,1)} collective-permute-done((bf16[512,2176]{0,1:T(8,128)(2,1)}, bf16[512,2176]{0,1:T(8,128)(2,1)}, u32[]{:S(2)}, u32[]{:S(2)}) %collective-permute-start.16) | collective-permute-done | bytes 2228256 | tf_op jit(solution)/shard_map/ppermute | solution.py:159
  118.6 0.8 slice.178
  120.1 2.7 convolution_convert_fusion.6
  122.9 1.4 fusion.13
  124.8 2.6 multiply_convert_fusion.4
  127.4 2.6 fusion.17
  130.0 2.2 fusion.2
  133.2 7.0 %all-to-all-start = ((f32[16,1,32]{2,1,0:T(1,128)}), f32[16,1,32]{2,1,0:T(1,128)S(1)}, u32[]{:S(2)}, u32[]{:S(2)}) async-start(f32[16,1,32]{2,1,0:T(1,128)} %bitcast.61), calls=%async_computation | async-start | bytes 16384 | tf_op jit(solution)/shard_map/all_to_all | solution.py:138
  140.3 2.9 %convolution_convert_fusion.2 = bf16[512,2048]{1,0:T(8,128)(2,1)S(1)} fusion(bf16[384,2048]{1,0:T(8,128)(2,1)} %copy-done.29, f32[384]{0:T(512)S(1)} %get-tuple-element.13, s32[512]{0:T(512)S(1)} %convert_element_type.217, pred[512]{0:T(512)(128)(4,1)S(1)} %broadcast_compare_fusion.2), kind=kOutput, calls=%fused_computation.21 | convolution fusion | flops 809107456 | bytes 3674112 | tf_op jit(solution)/shard_map/dot_general | solution.py:11
  143.2 1.3 copy-done.4
  144.5 1.1 select_bitcast_fusion.5
  145.9 2.5 multiply_convert_fusion.3
  148.4 3.2 %fusion.7 = f32[384,2048]{1,0:T(8,128)} fusion(bf16[384,768]{1,0:T(8,128)(2,1)S(1)} %get-tuple-element.18, bf16[1,2048,768]{2,1,0:T(8,128)(2,1)S(1)} %copy-done.26), kind=kOutput, calls=%fused_computation.11 | convolution fusion | flops 1207959552 | bytes 6881280 | tf_op jit(solution)/shard_map/dot_general | solution.py:11
  151.6 5.3 %convolution_convert_fusion.1 = bf16[512,2048]{1,0:T(8,128)(2,1)S(1)} fusion(f32[384,2048]{1,0:T(8,128)} %fusion.7, bf16[384,768]{1,0:T(8,128)(2,1)S(1)} %copy-done.14, bf16[1,2048,768]{2,1,0:T(8,128)(2,1)} %param.11, s32[512]{0:T(512)S(1)} %convert_element_type.217, pred[512]{0:T(512)(128)(4,1)S(1)} %broadcast_compare_fusion.2), kind=kOutput, calls=%fused_computation.20 | convolution fusion | flops 2016280576 | bytes 8980992 | tf_op jit(solution)/shard_map/dot_general | solution.py:11
  157.4 1.1 copy-done.17
  158.5 2.7 collective-permute-start.17
  161.7 2.8 %convolution_convert_fusion.3 = bf16[384,2048]{1,0:T(8,128)(2,1)S(1)} fusion(bf16[512,2176]{0,1:T(8,128)(2,1)} %collective-permute-done.16, s32[512]{0:T(512)S(1)} %convert_element_type.267, pred[512]{0:T(512)(128)(4,1)S(1)} %broadcast_compare_fusion), kind=kOutput, calls=%fused_computation.23 | convolution fusion | flops 806486016 | bytes 3672576 | tf_op jit(solution)/shard_map/dot_general | solution.py:11
  164.5 1.0 convolution_convert_fusion.4
  165.6 1.4 copy-done.7
  167.6 1.5 collective-permute-start.13
  169.2 1.7 fusion.28
  171.6 10.9 %collective-permute-done.13 = bf16[4,32,2048]{2,1,0:T(8,128)(2,1)S(1)} collective-permute-done((bf16[4,32,2048]{2,1,0:T(8,128)(2,1)S(1)}, bf16[4,32,2048]{2,1,0:T(8,128)(2,1)S(1)}, u32[]{:S(2)}, u32[]{:S(2)}) %collective-permute-start.13) | collective-permute-done | bytes 524320 | tf_op jit(solution)/shard_map/ppermute | solution.py:32
  182.8 1.5 collective-permute-start.14
  184.3 8.4 %collective-permute-done.5 = bf16[4,32,2048]{2,1,0:T(8,128)(2,1)S(1)} collective-permute-done((bf16[4,32,2048]{2,1,0:T(8,128)(2,1)S(1)}, bf16[4,32,2048]{2,1,0:T(8,128)(2,1)S(1)}, u32[]{:S(2)}, u32[]{:S(2)}) %collective-permute-start.5) | collective-permute-done | bytes 524320 | tf_op jit(solution)/shard_map/ppermute | solution.py:32
  193.0 1.5 collective-permute-start.6
  194.5 4.7 %collective-permute-done.14 = bf16[2,32,2048]{2,1,0:T(8,128)(2,1)S(1)} collective-permute-done((bf16[2,32,2048]{2,1,0:T(8,128)(2,1)S(1)}, bf16[2,32,2048]{2,1,0:T(8,128)(2,1)S(1)}, u32[]{:S(2)}, u32[]{:S(2)}) %collective-permute-start.14) | collective-permute-done | bytes 262176 | tf_op jit(solution)/shard_map/ppermute | solution.py:32
  199.5 22.2 %collective-permute-done.6 = bf16[2,32,2048]{2,1,0:T(8,128)(2,1)S(1)} collective-permute-done((bf16[2,32,2048]{2,1,0:T(8,128)(2,1)S(1)}, bf16[2,32,2048]{2,1,0:T(8,128)(2,1)S(1)}, u32[]{:S(2)}, u32[]{:S(2)}) %collective-permute-start.6) | collective-permute-done | bytes 262176 | tf_op jit(solution)/shard_map/ppermute | solution.py:32
  221.8 1.3 collective-permute-start.7
  223.1 0.7 fusion.86
  224.1 1.6 collective-permute-start.18
  225.7 5.2 %collective-permute-done.7 = bf16[1,32,2048]{2,1,0:T(8,128)(2,1)S(1)} collective-permute-done((bf16[1,32,2048]{2,1,0:T(8,128)(2,1)S(1)}, bf16[1,32,2048]{2,1,0:T(8,128)(2,1)S(1)}, u32[]{:S(2)}, u32[]{:S(2)}) %collective-permute-start.7) | collective-permute-done | bytes 131104 | tf_op jit(solution)/shard_map/ppermute | solution.py:32
  231.6 2.0 broadcast_select_fusion.1
  233.5 1.5 collective-permute-start.20
  236.6 28.0 %collective-permute-done.20 = bf16[384,768]{1,0:T(8,128)(2,1)} collective-permute-done((bf16[384,768]{1,0:T(8,128)(2,1)}, bf16[384,768]{1,0:T(8,128)(2,1)}, u32[]{:S(2)}, u32[]{:S(2)}) %collective-permute-start.20) | collective-permute-done | bytes 589856 | tf_op jit(solution)/shard_map/ppermute | solution.py:160
  264.6 3.8 %fusion.39 = bf16[1,768,1024]{2,1,0:T(8,128)(2,1)} fusion(bf16[384,1024]{1,0:T(8,128)(2,1)S(1)} %multiply_convert_fusion, bf16[384,1024]{1,0:T(8,128)(2,1)S(1)} %multiply_convert_fusion.1, bf16[384,768]{1,0:T(8,128)(2,1)} %collective-permute-done.20, bf16[384,768]{1,0:T(8,128)(2,1)} %broadcast_select_fusion.1), kind=kOutput, calls=%fused_computation.54 | convolution fusion | flops 1214251008 | bytes 4325376 | tf_op jit(solution)/shard_map/dot_general | solution.py:11
  268.4 4.3 %convolution_convert_fusion = bf16[1024,1536]{1,0:T(8,128)(2,1)S(1)} fusion(bf16[384,1536]{1,0:T(8,128)(2,1)} %collective-permute-done.18, bf16[384,1536]{1,0:T(8,128)(2,1)S(1)} %copy-done.21, bf16[384,1024]{1,0:T(8,128)(2,1)S(1)} %slice-done, bf16[384,1024]{1,0:T(8,128)(2,1)S(1)} %slice-done.1), kind=kOutput, calls=%fused_computation.3 | convolution fusion | flops 2425356288 | bytes 7077888 | tf_op jit(solution)/shard_map/dot_general | solution.py:11
  272.7 1.9 slice_bitcast_fusion
  (144 shorter events, 12.0 us)
Async XLA Ops:
  0.6 126.8 %copy-start = (bf16[1,768,2048]{2,1,0:T(8,128)(2,1)S(1)}, bf16[1,768,2048]{2,1,0:T(8,128)(2,1)}, u32[]{:S(2)}) copy-start(bf16[1,768,2048]{2,1,0:T(8,128)(2,1)} %param.13) | copy-start | bytes 9437188
  0.6 7.7 %collective-permute-start.8 = (bf16[32,2048]{1,0:T(8,128)(2,1)}, bf16[32,2048]{1,0:T(8,128)(2,1)S(1)}, u32[]{:S(2)}, u32[]{:S(2)}) collective-permute-start(bf16[32,2048]{1,0:T(8,128)(2,1)} %param.15), channel_id=1, source_target_pairs={{0,2},{1,3},{2,0},{3,1},{4,6},{5,7},{6,4},{7,5},{8,10},{9,11},{10,... | collective-permute-start | bytes 393224 | tf_op jit(solution)/shard_map/ppermute | solution.py:32
  5.7 9.2 %collective-permute-start = (bf16[32,2176]{1,0:T(8,128)(2,1)S(1)}, bf16[32,2176]{1,0:T(8,128)(2,1)S(1)}, u32[]{:S(2)}, u32[]{:S(2)}) collective-permute-start(bf16[32,2176]{1,0:T(8,128)(2,1)S(1)} %concatenate.24), channel_id=1, source_target_pairs={{0,8},{1,9},{2,10},{3,11},{4,12},{5,13},{6,14},{7,15},{8,0},{9,1},... | collective-permute-start | bytes 417800 | tf_op jit(solution)/shard_map/ppermute | solution.py:32
  9.3 10.9 %collective-permute-start.9 = (bf16[2,32,2048]{2,1,0:T(8,128)(2,1)S(1)}, bf16[2,32,2048]{2,1,0:T(8,128)(2,1)S(1)}, u32[]{:S(2)}, u32[]{:S(2)}) collective-permute-start(bf16[2,32,2048]{2,1,0:T(8,128)(2,1)S(1)} %pad_maximum_fusion.9), channel_id=1, source_target_pairs={{0,4},{1,5},{2,6},{3,7},{4,0},{5,1},{6,2},{7,3},{8,12},{9,13},{10,... | collective-permute-start | bytes 786440 | tf_op jit(solution)/shard_map/ppermute | solution.py:32
  14.9 14.1 %collective-permute-start.1 = (bf16[2,32,2176]{2,1,0:T(8,128)(2,1)S(1)}, bf16[2,32,2176]{2,1,0:T(8,128)(2,1)S(1)}, u32[]{:S(2)}, u32[]{:S(2)}) collective-permute-start(bf16[2,32,2176]{2,1,0:T(8,128)(2,1)S(1)} %pad_maximum_fusion.8), channel_id=1, source_target_pairs={{0,4},{1,5},{2,6},{3,7},{4,0},{5,1},{6,2},{7,3},{8,12},{9,13},{10,... | collective-permute-start | bytes 835592 | tf_op jit(solution)/shard_map/ppermute | solution.py:32
  20.3 23.2 %collective-permute-start.10 = (bf16[2,2,32,2048]{3,2,1,0:T(8,128)(2,1)S(1)}, bf16[2,2,32,2048]{3,2,1,0:T(8,128)(2,1)S(1)}, u32[]{:S(2)}, u32[]{:S(2)}) collective-permute-start(bf16[2,2,32,2048]{3,2,1,0:T(8,128)(2,1)S(1)} %pad_maximum_fusion.7), channel_id=1, source_target_pairs={{0,8},{1,9},{2,10},{3,11},{4,12},{5,13},{6,14},{7,15},{8,0},{9,1},... | collective-permute-start | bytes 1572872 | tf_op jit(solution)/shard_map/ppermute | solution.py:32
  29.1 15.7 %collective-permute-start.2 = (bf16[2,2,32,2176]{3,2,1,0:T(8,128)(2,1)S(1)}, bf16[2,2,32,2176]{3,2,1,0:T(8,128)(2,1)S(1)}, u32[]{:S(2)}, u32[]{:S(2)}) collective-permute-start(bf16[2,2,32,2176]{3,2,1,0:T(8,128)(2,1)S(1)} %pad_maximum_fusion.6), channel_id=1, source_target_pairs={{0,2},{1,3},{2,0},{3,1},{4,6},{5,7},{6,4},{7,5},{8,10},{9,11},{10,... | collective-permute-start | bytes 1671176 | tf_op jit(solution)/shard_map/ppermute | solution.py:32
  43.6 1.3 copy-start.12
  43.6 1.3 copy-start.13
  44.8 3.0 %collective-permute-start.11 = (bf16[2,2,2,32,2048]{4,3,2,1,0:T(8,128)(2,1)}, bf16[2,2,2,32,2048]{4,3,2,1,0:T(8,128)(2,1)}, u32[]{:S(2)}, u32[]{:S(2)}) collective-permute-start(bf16[2,2,2,32,2048]{4,3,2,1,0:T(8,128)(2,1)} %pad_maximum_fusion.5), channel_id=1, source_target_pairs={{0,1},{1,0},{2,3},{3,2},{4,5},{5,4},{6,7},{7,6},{8,9},{9,8},{10,11... | collective-permute-start | bytes 3145736 | tf_op jit(solution)/shard_map/ppermute | solution.py:32
  44.9 0.8 copy-start.8
  44.9 1.9 copy-start.10
  46.8 4.1 %collective-permute-start.3 = (bf16[2,2,2,32,2176]{4,3,2,1,0:T(8,128)(2,1)}, bf16[2,2,2,32,2176]{4,3,2,1,0:T(8,128)(2,1)}, u32[]{:S(2)}, u32[]{:S(2)}) collective-permute-start(bf16[2,2,2,32,2176]{4,3,2,1,0:T(8,128)(2,1)} %pad_maximum_fusion.4), channel_id=1, source_target_pairs={{0,1},{1,0},{2,3},{3,2},{4,5},{5,4},{6,7},{7,6},{8,9},{9,8},{10,11... | collective-permute-start | bytes 3342344 | tf_op jit(solution)/shard_map/ppermute | solution.py:32
  49.4 1.5 copy-start.9
  49.5 1.5 copy-start.11
  52.7 1.4 copy-start.2
  64.7 4.6 %copy-start.28 = (s32[16]{0:T(128)S(1)}, s32[16]{0:T(128)}, u32[]{:S(2)}) copy-start(s32[16]{0:T(128)} %param.14) | copy-start | bytes 196
  67.8 50.8 %collective-permute-start.16 = (bf16[512,2176]{0,1:T(8,128)(2,1)}, bf16[512,2176]{0,1:T(8,128)(2,1)}, u32[]{:S(2)}, u32[]{:S(2)}) collective-permute-start(bf16[512,2176]{0,1:T(8,128)(2,1)} %pad_maximum_fusion.1), channel_id=1, source_target_pairs={{0,16},{16,0},{1,17},{17,1},{2,18},{18,2},{3,19},{19,3},{4,20},{20... | collective-permute-start | bytes 6684680 | tf_op jit(solution)/shard_map/ppermute | solution.py:159
  120.1 2.8 %copy-start.27 = (bf16[1,2048,768]{2,1,0:T(8,128)(2,1)S(1)}, bf16[1,2048,768]{2,1,0:T(8,128)(2,1)}, u32[]{:S(2)}) copy-start(bf16[1,2048,768]{2,1,0:T(8,128)(2,1)} %param.11) | copy-start | bytes 9437188
  122.9 1.9 copy-start.25
  124.8 2.6 copy-start.31
  127.4 2.6 copy-start.3
  127.4 104.2 %collective-permute-start.19 = (bf16[384,768]{1,0:T(8,128)(2,1)}, bf16[384,768]{1,0:T(8,128)(2,1)}, u32[]{:S(2)}, u32[]{:S(2)}) collective-permute-start(bf16[384,768]{1,0:T(8,128)(2,1)} %get-tuple-element.42), channel_id=1, source_target_pairs={{0,8},{1,9},{2,10},{3,11},{4,12},{5,13},{6,14},{7,15},{8,0},{9,1},... | collective-permute-start | bytes 1769480 | tf_op jit(solution)/shard_map/ppermute | solution.py:127
  130.0 2.2 copy-start.29
  133.2 102.3 %all-to-all-start = ((f32[16,1,32]{2,1,0:T(1,128)}), f32[16,1,32]{2,1,0:T(1,128)S(1)}, u32[]{:S(2)}, u32[]{:S(2)}) async-start(f32[16,1,32]{2,1,0:T(1,128)} %bitcast.61), calls=%async_computation | async-start | bytes 16384 | tf_op jit(solution)/shard_map/all_to_all | solution.py:138
  140.3 5.6 %copy-start.33 = (f32[384,768]{1,0:T(8,128)S(1)}, f32[384,768]{1,0:T(8,128)}, u32[]{:S(2)}) copy-start(f32[384,768]{1,0:T(8,128)} %get-tuple-element.43) | copy-start | bytes 3538948
  143.2 1.4 copy-start.4
  143.2 2.7 copy-start.30
  143.2 2.7 copy-start.32
  145.6 23.6 %collective-permute-start.4 = (bf16[8,32,2048]{2,1,0:T(8,128)(2,1)}, bf16[8,32,2048]{2,1,0:T(8,128)(2,1)}, u32[]{:S(2)}, u32[]{:S(2)}) collective-permute-start(bf16[8,32,2048]{2,1,0:T(8,128)(2,1)} %select_bitcast_fusion.5), channel_id=1, source_target_pairs={{0,1},{1,0},{2,3},{3,2},{4,5},{5,4},{6,7},{7,6},{8,9},{9,8},{10,11... | collective-permute-start | bytes 3145736 | tf_op jit(solution)/shard_map/ppermute | solution.py:32
  145.9 2.5 copy-start.26
  148.4 3.2 %copy-start.16 = (bf16[384,768]{1,0:T(8,128)(2,1)}, bf16[384,768]{1,0:T(8,128)(2,1)S(1)}, u32[]{:S(2)}) copy-start(bf16[384,768]{1,0:T(8,128)(2,1)S(1)} %get-tuple-element.18) | copy-start | bytes 1769476
  148.4 3.2 %copy-start.14 = (bf16[384,768]{1,0:T(8,128)(2,1)S(1)}, bf16[384,768]{1,0:T(8,128)(2,1)}, u32[]{:S(2)}) copy-start(bf16[384,768]{1,0:T(8,128)(2,1)} %get-tuple-element.17) | copy-start | bytes 1769476
  156.9 1.6 copy-start.6
  156.9 1.5 copy-start.17
  157.1 8.5 %collective-permute-start.12 = (bf16[8,32,2048]{2,1,0:T(8,128)(2,1)S(1)}, bf16[8,32,2048]{2,1,0:T(8,128)(2,1)S(1)}, u32[]{:S(2)}, u32[]{:S(2)}) collective-permute-start(bf16[8,32,2048]{2,1,0:T(8,128)(2,1)S(1)} %select_bitcast_fusion.2), channel_id=1, source_target_pairs={{0,1},{1,0},{2,3},{3,2},{4,5},{5,4},{6,7},{7,6},{8,9},{9,8},{10,11... | collective-permute-start | bytes 3145736 | tf_op jit(solution)/shard_map/ppermute | solution.py:32
  158.5 65.3 %collective-permute-start.17 = (bf16[384,1536]{1,0:T(8,128)(2,1)S(1)}, bf16[384,1536]{1,0:T(8,128)(2,1)S(1)}, u32[]{:S(2)}, u32[]{:S(2)}) collective-permute-start(bf16[384,1536]{1,0:T(8,128)(2,1)S(1)} %pad_maximum_fusion.3), channel_id=1, source_target_pairs={{0,8},{1,9},{2,10},{3,11},{4,12},{5,13},{6,14},{7,15},{8,0},{9,1},... | collective-permute-start | bytes 3538952 | tf_op jit(solution)/shard_map/ppermute | solution.py:128
  161.7 2.8 %copy-start.22 = (bf16[512,1024]{0,1:T(8,128)(2,1)S(1)}, bf16[512,1024]{0,1:T(8,128)(2,1)}, u32[]{:S(2)}) copy-start(bf16[512,1024]{0,1:T(8,128)(2,1)} %copy.167) | copy-start | bytes 3145732
  161.7 2.8 %copy-start.23 = (bf16[512,1024]{0,1:T(8,128)(2,1)S(1)}, bf16[512,1024]{0,1:T(8,128)(2,1)}, u32[]{:S(2)}) copy-start(bf16[512,1024]{0,1:T(8,128)(2,1)} %copy.170) | copy-start | bytes 3145732
  164.5 71.0 %copy-start.18 = (bf16[384,2048]{1,0:T(8,128)(2,1)}, bf16[384,2048]{1,0:T(8,128)(2,1)S(1)}, u32[]{:S(2)}) copy-start(bf16[384,2048]{1,0:T(8,128)(2,1)S(1)} %convolution_convert_fusion.3) | copy-start | bytes 4718596
  164.5 2.5 copy-start.7
  165.6 69.9 %copy-start.19 = (bf16[384,2048]{1,0:T(8,128)(2,1)}, bf16[384,2048]{1,0:T(8,128)(2,1)S(1)}, u32[]{:S(2)}) copy-start(bf16[384,2048]{1,0:T(8,128)(2,1)S(1)} %convolution_convert_fusion.4) | copy-start | bytes 4718596
  165.6 3.6 %copy-start.5 = (bf16[512,2048]{1,0:T(8,128)(2,1)S(1)}, bf16[512,2048]{1,0:T(8,128)(2,1)}, u32[]{:S(2)}) copy-start(bf16[512,2048]{1,0:T(8,128)(2,1)} %copy-done.4) | copy-start | bytes 6291460
  167.6 14.9 %collective-permute-start.13 = (bf16[4,32,2048]{2,1,0:T(8,128)(2,1)S(1)}, bf16[4,32,2048]{2,1,0:T(8,128)(2,1)S(1)}, u32[]{:S(2)}, u32[]{:S(2)}) collective-permute-start(bf16[4,32,2048]{2,1,0:T(8,128)(2,1)S(1)} %select_bitcast_fusion.8), channel_id=1, source_target_pairs={{0,2},{1,3},{2,0},{3,1},{4,6},{5,7},{6,4},{7,5},{8,10},{9,11},{10,... | collective-permute-start | bytes 1572872 | tf_op jit(solution)/shard_map/ppermute | solution.py:32
  171.0 21.7 %collective-permute-start.5 = (bf16[4,32,2048]{2,1,0:T(8,128)(2,1)S(1)}, bf16[4,32,2048]{2,1,0:T(8,128)(2,1)S(1)}, u32[]{:S(2)}, u32[]{:S(2)}) collective-permute-start(bf16[4,32,2048]{2,1,0:T(8,128)(2,1)S(1)} %fusion.63), channel_id=1, source_target_pairs={{0,2},{1,3},{2,0},{3,1},{4,6},{5,7},{6,4},{7,5},{8,10},{9,11},{10,... | collective-permute-start | bytes 1572872 | tf_op jit(solution)/shard_map/ppermute | solution.py:32
  182.8 16.5 %collective-permute-start.14 = (bf16[2,32,2048]{2,1,0:T(8,128)(2,1)S(1)}, bf16[2,32,2048]{2,1,0:T(8,128)(2,1)S(1)}, u32[]{:S(2)}, u32[]{:S(2)}) collective-permute-start(bf16[2,32,2048]{2,1,0:T(8,128)(2,1)S(1)} %select_bitcast_fusion.13), channel_id=1, source_target_pairs={{0,4},{1,5},{2,6},{3,7},{4,0},{5,1},{6,2},{7,3},{8,12},{9,13},{10,... | collective-permute-start | bytes 786440 | tf_op jit(solution)/shard_map/ppermute | solution.py:32
  193.0 30.9 %copy-start.15 = (bf16[384,768]{1,0:T(8,128)(2,1)S(1)}, bf16[384,768]{1,0:T(8,128)(2,1)}, u32[]{:S(2)}) copy-start(bf16[384,768]{1,0:T(8,128)(2,1)} %get-tuple-element.17) | copy-start | bytes 1769476
  193.0 28.6 %collective-permute-start.6 = (bf16[2,32,2048]{2,1,0:T(8,128)(2,1)S(1)}, bf16[2,32,2048]{2,1,0:T(8,128)(2,1)S(1)}, u32[]{:S(2)}, u32[]{:S(2)}) collective-permute-start(bf16[2,32,2048]{2,1,0:T(8,128)(2,1)S(1)} %fusion.79), channel_id=1, source_target_pairs={{0,4},{1,5},{2,6},{3,7},{4,0},{5,1},{6,2},{7,3},{8,12},{9,13},{10,... | collective-permute-start | bytes 786440 | tf_op jit(solution)/shard_map/ppermute | solution.py:32
  199.4 23.7 %collective-permute-start.15 = (bf16[1,32,2048]{2,1,0:T(8,128)(2,1)S(1)}, bf16[1,32,2048]{2,1,0:T(8,128)(2,1)S(1)}, u32[]{:S(2)}, u32[]{:S(2)}) collective-permute-start(bf16[1,32,2048]{2,1,0:T(8,128)(2,1)S(1)} %select_bitcast_fusion.18), channel_id=1, source_target_pairs={{0,8},{1,9},{2,10},{3,11},{4,12},{5,13},{6,14},{7,15},{8,0},{9,1},... | collective-permute-start | bytes 393224 | tf_op jit(solution)/shard_map/ppermute | solution.py:32
  221.8 9.1 %collective-permute-start.7 = (bf16[1,32,2048]{2,1,0:T(8,128)(2,1)S(1)}, bf16[1,32,2048]{2,1,0:T(8,128)(2,1)S(1)}, u32[]{:S(2)}, u32[]{:S(2)}) collective-permute-start(bf16[1,32,2048]{2,1,0:T(8,128)(2,1)S(1)} %select_bitcast_fusion.21), channel_id=1, source_target_pairs={{0,8},{1,9},{2,10},{3,11},{4,12},{5,13},{6,14},{7,15},{8,0},{9,1},... | collective-permute-start | bytes 393224 | tf_op jit(solution)/shard_map/ppermute | solution.py:32
  224.1 11.4 %copy-start.20 = (bf16[384,1536]{1,0:T(8,128)(2,1)}, bf16[384,1536]{1,0:T(8,128)(2,1)S(1)}, u32[]{:S(2)}) copy-start(bf16[384,1536]{1,0:T(8,128)(2,1)S(1)} %broadcast_select_fusion) | copy-start | bytes 3538948
  224.1 44.2 %collective-permute-start.18 = (bf16[384,1536]{1,0:T(8,128)(2,1)S(1)}, bf16[384,1536]{1,0:T(8,128)(2,1)}, u32[]{:S(2)}, u32[]{:S(2)}) collective-permute-start(bf16[384,1536]{1,0:T(8,128)(2,1)S(1)} %broadcast_select_fusion), channel_id=1, source_target_pairs={{0,16},{16,0},{1,17},{17,1},{2,18},{18,2},{3,19},{19,3},{4,20},{20... | collective-permute-start | bytes 3538952 | tf_op jit(solution)/shard_map/ppermute | solution.py:161
  233.5 31.0 %collective-permute-start.20 = (bf16[384,768]{1,0:T(8,128)(2,1)}, bf16[384,768]{1,0:T(8,128)(2,1)}, u32[]{:S(2)}, u32[]{:S(2)}) collective-permute-start(bf16[384,768]{1,0:T(8,128)(2,1)} %broadcast_select_fusion.1), channel_id=1, source_target_pairs={{0,16},{16,0},{1,17},{17,1},{2,18},{18,2},{3,19},{19,3},{4,20},{20... | collective-permute-start | bytes 1769480 | tf_op jit(solution)/shard_map/ppermute | solution.py:160
  235.3 0.7 copy-start.24
  236.6 31.8 %slice-start = ((bf16[384,2048]{1,0:T(8,128)(2,1)}), bf16[384,1024]{1,0:T(8,128)(2,1)S(1)}, s32[]{:S(2)}) async-start(bf16[384,2048]{1,0:T(8,128)(2,1)} %copy-done.18), calls=%async_computation.1 | async-start | bytes 1572864 | tf_op jit(solution)/shard_map/slice | solution.py:164
  236.6 31.8 %slice-start.1 = ((bf16[384,2048]{1,0:T(8,128)(2,1)}), bf16[384,1024]{1,0:T(8,128)(2,1)S(1)}, s32[]{:S(2)}) async-start(bf16[384,2048]{1,0:T(8,128)(2,1)} %copy-done.19), calls=%async_computation.2 | async-start | bytes 1572864 | tf_op jit(solution)/shard_map/slice | solution.py:164
  236.6 31.8 %copy-start.21 = (bf16[384,1536]{1,0:T(8,128)(2,1)S(1)}, bf16[384,1536]{1,0:T(8,128)(2,1)}, u32[]{:S(2)}) copy-start(bf16[384,1536]{1,0:T(8,128)(2,1)} %copy-done.20) | copy-start | bytes 3538948
  268.4 6.2 %copy-start.1 = (bf16[1,768,2048]{2,1,0:T(8,128)(2,1)S(1)}, bf16[1,768,2048]{2,1,0:T(8,128)(2,1)}, u32[]{:S(2)}) copy-start(bf16[1,768,2048]{2,1,0:T(8,128)(2,1)} %param.13) | copy-start | bytes 9437188

commit v3 on v2

--- a/solution.py
+++ b/solution.py
@@ -78,7 +78,6 @@
     group = lax.axis_index("dp")
     tok_count, width = tokens.shape
     top = routes.shape[1]
-    ff = w_gate.shape[2]
     part = width // groups
     rows = experts * tok_count
     capacity = experts * min(
@@ -123,16 +122,18 @@
     half = experts // 2
     trade = [(i, (i + half) % experts) for i in range(experts)]
 
-    pres = jnp.concatenate([d_gate_pre, d_up_pre], axis=1)
     far_hidden = lax.ppermute(hidden, "expert", trade)
-    far_pres = lax.ppermute(pres, "expert", trade)
+    far_gate = lax.ppermute(d_gate_pre, "expert", trade)
+    far_up = lax.ppermute(d_up_pre, "expert", trade)
 
-    result = dot(hidden, down_mat, 1, 0).astype(BF16)
+    result = dot(after(hidden, d_gate_pre, d_up_pre), down_mat, 1, 0).astype(BF16)
     result_f = result.astype(F32)
     mixed = (weight * result_f).astype(BF16)
     mixture = scatter_sum(dot(picks, mixed, 0, 0).astype(BF16), bits)
     d_rows = (dot(d_gate_pre, gate_mat, 1, 1) + dot(d_up_pre, up_mat, 1, 1)).astype(BF16)
-    d_tokens = scatter_sum(dot(picks, d_rows, 0, 0).astype(BF16), bits)
+    d_spread = dot(picks, d_rows, 0, 0).astype(BF16)
+    d_tokens = scatter_sum(d_spread, bits)
+    result_f = after(result, d_tokens).astype(F32)
     inner = jnp.sum(result_f * cot.astype(F32), axis=1, keepdims=True)
     inner = jnp.sum(picks.astype(F32) * inner, axis=0).reshape(experts, tok_count)
     inner = lax.all_to_all(inner, "expert", split_axis=0, concat_axis=0, tiled=True)
@@ -142,32 +143,37 @@
 
     placed = jnp.where(swapped, (own + half) % experts, own)
     acts = (
-        jnp.where(swapped, after(far_hidden, mixture), hidden),
-        jnp.where(swapped, after(far_pres, d_tokens), pres),
+        jnp.where(swapped, after(far_hidden, d_spread), hidden),
+        jnp.where(swapped, after(far_gate, mixture), d_gate_pre),
+        jnp.where(swapped, after(far_up, d_tokens), d_up_pre),
     )
-    xs, cots, hiddens, pre_parts = [], [], [], []
+    late_tokens, late_d_out, late_table = lax.optimization_barrier(
+        (tokens_all, d_out_all, table, d_gate_pre, d_up_pre)
+    )[:3]
+    xs, cots, acts_of = [], [], []
     for shift in range(groups):
         target = (group + shift) % groups
         block = jnp.concatenate(
-            [lax.dynamic_slice_in_dim(a, target * part, part, 1) for a in (tokens_all, d_out_all)]
-            + [table],
+            [lax.dynamic_slice_in_dim(a, target * part, part, 1) for a in (late_tokens, late_d_out)]
+            + [late_table],
             axis=1,
         )
-        h, pre = acts
+        parts = acts
         if shift:
             ring = [(i, (i + shift) % groups) for i in range(groups)]
-            block = lax.ppermute(block, "dp", ring)
-            h = lax.ppermute(h, "dp", ring)
-            pre = lax.ppermute(pre, "dp", ring)
+            block = after(lax.ppermute(block, "dp", ring), mixture)
+            parts = [lax.ppermute(a, "dp", ring) for a in acts]
         choose, scale = row_picker(column_of(block[:, 2 * part :], placed), capacity)
         chosen = dot(choose, block[:, : 2 * part], 1, 0).astype(BF16)
         xs.append(chosen[:, :part])
         cots.append((scale * chosen[:, part:].astype(F32)).astype(BF16))
-        hiddens.append(h)
-        pre_parts.append(pre)
-    g_pre = dot(jnp.concatenate(xs), jnp.concatenate(pre_parts), 0, 0).astype(BF16)
-    g_down = dot(jnp.concatenate(hiddens), jnp.concatenate(cots), 0, 0).astype(BF16)
-    return (mixture, d_tokens, d_gates, g_pre[None, :, :ff], g_pre[None, :, ff:], g_down[None])
+        acts_of.append(parts)
+    x, cot = jnp.concatenate(xs), jnp.concatenate(cots)
+    hidden, d_gate_pre, d_up_pre = (jnp.concatenate(a) for a in zip(*acts_of))
+    g_down = dot(hidden, cot, 0, 0).astype(BF16)
+    g_gate = dot(x, d_gate_pre, 0, 0).astype(BF16)
+    g_up = dot(x, d_up_pre, 0, 0).astype(BF16)
+    return (mixture, d_tokens, d_gates, g_gate[None], g_up[None], g_down[None])
 
 
 def solution(mesh):

time: 275 us -> 250 us (0.909)
  waiting for transfers between devices: 152 us -> 131 us
  local copies, waits for them, and re-layouts: 28.6 us -> 20.3 us
  other arithmetic: 22.4 us -> 29.1 us
  starting transfers between devices: 31.8 us -> 25.1 us
  matrix products: 37.9 us -> 41.4 us
    ppermute x4 -> x6, waiting for transfers between devices: 70.4 us -> 10.1 us  [the longest x3 10.1 us: on_device(): parts = [lax.ppermute(a, 'dp', ring) for a in acts]]
    ppermute x1, waiting for transfers between devices: 0.01 us -> 47.9 us  [on_device(): far_hidden = lax.ppermute(hidden, 'expert', trade)]
    unnamed x75 -> x50, local copies, waits for them, and re-layouts: 18.1 us -> 6.8 us
    ppermute x16, waiting for transfers between devices: 81.6 us -> 72.8 us  [swap_bit(): lax.ppermute(value, 'expert', [(i, i ^ 1 << bit) for i in range(size)])]
    optimization_barrier x0 -> x3, local copies, waits for them, and re-layouts: none -> 6.9 us  [on_device(): lax.optimization_barrier((tokens_all, d_out_all, table, d_gate_pre, d_up_...]
    ppermute x16, starting transfers between devices: 17.4 us -> 13.2 us  [swap_bit(): lax.ppermute(value, 'expert', [(i, i ^ 1 << bit) for i in range(size)])]
    select_n x2 -> x3, other arithmetic: 2.25 us -> 5.88 us  [the longest x1 1.98 us: on_device(): jnp.where(swapped, after(far_up, d_tokens), d_up_pre)]
    dot_general x16 -> x17, matrix products: 37.9 us -> 41.4 us  [dot(): lax.dot_general(left, right, (((lhs_dim,), (rhs_dim,)), ((), ())), prefer...]
  transfers between devices with their start and end apart: 22 -> 24, of which waited for: 12 -> 12; matrix products, arithmetic and copies ran while one was open for 19% -> 25% of each run, Pallas kernels for 0% -> 0%
where the time goes in v3:
time: 250 us; the launch traced here: 249 us
  waiting for transfers between devices  131 us (52%)
  matrix products  41.4 us (17%)
  other arithmetic  29.1 us (12%)
  starting transfers between devices  25.1 us (10%)
  local copies, waits for them, and re-layouts  20.3 us (8%)
    ppermute x16, waiting for transfers between devices, swap_bit(): lax.ppermute(value, 'expert', [(i, i ^ 1 << bit) for i in range(size)])  72.8 us
    ppermute x1, waiting for transfers between devices, on_device(): far_hidden = lax.ppermute(hidden, 'expert', trade)  47.9 us
    dot_general x17, matrix products, dot(): lax.dot_general(left, right, (((lhs_dim,), (rhs_dim,)), ((), ())), prefer...  41.4 us
    ppermute x16, starting transfers between devices, swap_bit(): lax.ppermute(value, 'expert', [(i, i ^ 1 << bit) for i in range(size)])  13.2 us
    ppermute x3, waiting for transfers between devices, on_device(): parts = [lax.ppermute(a, 'dp', ring) for a in acts]  10.1 us
    another operation x16, other arithmetic, gather_rows(): jnp.stack([jnp.where(high, other, held), jnp.where(high, held, other)], a...  8.62 us
    optimization_barrier x3, local copies, waits for them, and re-layouts, on_device(): lax.optimization_barrier((tokens_all, d_out_all, table, d_gate_pre, d_up_...  6.9 us
    unnamed x50, local copies, waits for them, and re-layouts  6.8 us
  transfers between devices with their start and end apart: 24, of which 12 were waited for; matrix products, arithmetic and copies ran while one was open for 25% of the time, Pallas kernels for 0%

profile of v3, /device:TPU:0, one launch (start us, length us, event | category | flops | bytes accessed | tf_op | source)
XLA Modules:
  0.0 248.7 jit_solution(18442733651881072948)
XLA Ops:
  0.6 3.0 %collective-permute-start.4 = (bf16[32,2048]{1,0:T(8,128)(2,1)}, bf16[32,2048]{1,0:T(8,128)(2,1)S(1)}, u32[]{:S(2)}, u32[]{:S(2)}) collective-permute-start(bf16[32,2048]{1,0:T(8,128)(2,1)} %param.15), channel_id=1, source_target_pairs={{0,2},{1,3},{2,0},{3,1},{4,6},{5,7},{6,4},{7,5},{8,10},{9,11},{10,... | collective-permute-start | bytes 393224 | tf_op jit(solution)/shard_map/ppermute | solution.py:32
  3.7 0.7 select_reduce_fusion.4
  4.7 1.0 concatenate.24
  5.7 2.6 %collective-permute-start = (bf16[32,2176]{1,0:T(8,128)(2,1)S(1)}, bf16[32,2176]{1,0:T(8,128)(2,1)S(1)}, u32[]{:S(2)}, u32[]{:S(2)}) collective-permute-start(bf16[32,2176]{1,0:T(8,128)(2,1)S(1)} %concatenate.24), channel_id=1, source_target_pairs={{0,8},{1,9},{2,10},{3,11},{4,12},{5,13},{6,14},{7,15},{8,0},{9,1},... | collective-permute-start | bytes 417800 | tf_op jit(solution)/shard_map/ppermute | solution.py:32
  8.3 0.9 select_bitcast_fusion.21
  9.3 1.6 collective-permute-start.5
  10.9 3.9 %collective-permute-done = bf16[32,2176]{1,0:T(8,128)(2,1)S(1)} collective-permute-done((bf16[32,2176]{1,0:T(8,128)(2,1)S(1)}, bf16[32,2176]{1,0:T(8,128)(2,1)S(1)}, u32[]{:S(2)}, u32[]{:S(2)}) %collective-permute-start) | collective-permute-done | bytes 139296 | tf_op jit(solution)/shard_map/ppermute | solution.py:32
  15.6 4.6 %collective-permute-done.5 = bf16[2,32,2048]{2,1,0:T(8,128)(2,1)S(1)} collective-permute-done((bf16[2,32,2048]{2,1,0:T(8,128)(2,1)S(1)}, bf16[2,32,2048]{2,1,0:T(8,128)(2,1)S(1)}, u32[]{:S(2)}, u32[]{:S(2)}) %collective-permute-start.5) | collective-permute-done | bytes 262176 | tf_op jit(solution)/shard_map/ppermute | solution.py:32
  20.3 1.5 collective-permute-start.6
  21.8 7.2 %collective-permute-done.1 = bf16[2,32,2176]{2,1,0:T(8,128)(2,1)S(1)} collective-permute-done((bf16[2,32,2176]{2,1,0:T(8,128)(2,1)S(1)}, bf16[2,32,2176]{2,1,0:T(8,128)(2,1)S(1)}, u32[]{:S(2)}, u32[]{:S(2)}) %collective-permute-start.1) | collective-permute-done | bytes 278560 | tf_op jit(solution)/shard_map/ppermute | solution.py:32
  29.4 14.1 %collective-permute-done.6 = bf16[2,2,32,2048]{3,2,1,0:T(8,128)(2,1)S(1)} collective-permute-done((bf16[2,2,32,2048]{3,2,1,0:T(8,128)(2,1)S(1)}, bf16[2,2,32,2048]{3,2,1,0:T(8,128)(2,1)S(1)}, u32[]{:S(2)}, u32[]{:S(2)}) %collective-permute-start.6) | collective-permute-done | bytes 524320 | tf_op jit(solution)/shard_map/ppermute | solution.py:32
  43.6 1.2 pad_maximum_fusion.5
  45.0 0.8 copy-done.8
  45.8 1.1 pad_maximum_fusion.4
  48.7 1.7 select_bitcast_fusion.5
  50.4 1.5 pad_maximum_fusion.2
  51.9 1.5 select_bitcast_fusion.1
  53.7 1.4 copy-done.2
  55.5 2.7 %convolution_convert_fusion.5 = bf16[384,2048]{1,0:T(8,128)(2,1)S(1)} fusion(s32[512]{0:T(512)S(1)} %convert_element_type.223, pred[512]{0:T(512)(128)(4,1)S(1)} %broadcast_compare_fusion.2, bf16[512,2176]{1,0:T(8,128)(2,1)} %bitcast.247), kind=kOutput, calls=%fused_computation.24 | convolution fusion | flops 806486016 | bytes 3672576 | tf_op jit(solution)/shard_map/dot_general | solution.py:11
  58.5 1.6 slice.163
  60.1 1.0 copy-done.22
  61.1 1.4 fusion.12
  63.0 1.4 fusion.8
  64.6 1.0 convolution_convert_fusion.4
  65.6 3.0 %multiply_convert_fusion.4 = (bf16[384,768]{1,0:T(8,128)(2,1)}, bf16[384,768]{1,0:T(8,128)(2,1)}, bf16[384,768]{1,0:T(8,128)(2,1)}) fusion(f32[384,768]{1,0:T(8,128)S(1)} %fusion.12, f32[384,768]{1,0:T(8,128)S(1)} %fusion.8, bf16[1,768,2048]{2,1,0:T(8,128)(2,1)S(1)} %copy-done, bf16[384,2048]{1,0:T(8,128)(2,1)S(1)} %convolution_convert_fusion.4, ...), kind=kOutput, calls=%fused_computation.59 | convolution fusion | flops 1214742528 | bytes 8848896 | tf_op jit(solution)/shard_map/dot_general | solution.py:11
  68.7 4.1 %fusion.6 = f32[384,2048]{1,0:T(8,128)} fusion(bf16[384,768]{1,0:T(8,128)(2,1)} %get-tuple-element.26, bf16[1,2048,768]{2,1,0:T(8,128)(2,1)S(1)} %copy-done.21), kind=kOutput, calls=%fused_computation.8 | convolution fusion | flops 1207959552 | bytes 6881280 | tf_op jit(solution)/shard_map/dot_general | solution.py:11
  72.8 2.9 %collective-permute-start.17 = (bf16[384,768]{1,0:T(8,128)(2,1)}, bf16[384,768]{1,0:T(8,128)(2,1)}, u32[]{:S(2)}, u32[]{:S(2)}) collective-permute-start(bf16[384,768]{1,0:T(8,128)(2,1)} %get-tuple-element.27), channel_id=1, source_target_pairs={{0,8},{1,9},{2,10},{3,11},{4,12},{5,13},{6,14},{7,15},{8,0},{9,1},... | collective-permute-start | bytes 1769480 | tf_op jit(solution)/shard_map/ppermute | solution.py:126
  75.8 2.5 fusion.16
  78.3 1.1 copy-done.16
  79.4 1.6 convolution_convert_fusion.1
  81.0 7.7 %convolution_convert_fusion = bf16[512,2048]{1,0:T(8,128)(2,1)} fusion(f32[384,2048]{1,0:T(8,128)} %fusion.6, bf16[384,768]{1,0:T(8,128)(2,1)} %get-tuple-element.27, bf16[1,2048,768]{2,1,0:T(8,128)(2,1)} %param.11, s32[512]{0:T(512)S(1)} %convert_element_type.223, pred[512]{0:T(512)(128)(4,1)S(1)} %broadcast_compare_fusion.2), kind=kOutput, calls=%fused_computation.18 | convolution fusion | flops 2016280576 | bytes 8980992 | tf_op jit(solution)/shard_map/dot_general | solution.py:11
  88.7 2.6 %select_bitcast_fusion.2 = bf16[8,32,2048]{2,1,0:T(8,128)(2,1)} fusion(pred[]{:T(512)S(6)} %eq.126, bf16[8,2,32,2048]{3,2,1,0:T(8,128)(2,1)} %bitcast.258), kind=kLoop, calls=%fused_computation.76 | loop fusion | flops 524288 | bytes 3145729 | tf_op jit(solution)/shard_map/jit(_where)/select_n | solution.py:56
  91.3 1.1 select_bitcast_fusion.3
  92.9 2.9 %copy.160 = bf16[512,2048]{0,1:T(8,128)(2,1)S(1)} copy(bf16[512,2048]{1,0:T(8,128)(2,1)} %slice.163) | data formatting | bytes 4194304 | tf_op jit(solution)/shard_map/optimization_barrier | solution.py:150
  95.9 3.9 %copy.157 = bf16[512,2048]{0,1:T(8,128)(2,1)} copy(bf16[512,2048]{1,0:T(8,128)(2,1)} %bitcast.254) | data formatting | bytes 4194304 | tf_op jit(solution)/shard_map/optimization_barrier | solution.py:150
  99.9 3.1 %constant_dynamic-slice_fusion.2 = (bf16[512,1024]{0,1:T(8,128)(2,1)}, bf16[512,1024]{0,1:T(8,128)(2,1)S(1)}, bf16[512,1024]{0,1:T(8,128)(2,1)S(1)}, bf16[512,1024]{0,1:T(8,128)(2,1)}) fusion(bf16[512,2048]{0,1:T(8,128)(2,1)} %copy.157, s32[]{:T(128)S(6)} %select_n.442, s32[]{:T(128)S(6)} %select_n.444, bf16[512,2048]{0,1:T(8,128)(2,1)S(1)} %copy.160), kind=kLoop, calls=%fused_computation.183 | loop fusion | bytes 8388616 | tf_op jit(solution)/shard_map/dynamic_slice | solution.py:157
  103.0 1.5 pad_maximum_fusion.1
  104.5 47.9 %collective-permute-done.21 = bf16[384,768]{1,0:T(8,128)(2,1)} collective-permute-done((bf16[384,768]{1,0:T(8,128)(2,1)}, bf16[384,768]{1,0:T(8,128)(2,1)}, u32[]{:S(2)}, u32[]{:S(2)}) %collective-permute-start.21) | collective-permute-done | bytes 589856 | tf_op jit(solution)/shard_map/ppermute | solution.py:125
  152.4 1.5 collective-permute-start.16
  154.0 1.9 broadcast_select_fusion
  156.4 1.9 fusion.22
  158.4 1.1 collective-permute-start.13
  159.5 1.7 fusion.23
  161.3 9.5 %collective-permute-done.13 = bf16[4,32,2048]{2,1,0:T(8,128)(2,1)S(1)} collective-permute-done((bf16[4,32,2048]{2,1,0:T(8,128)(2,1)S(1)}, bf16[4,32,2048]{2,1,0:T(8,128)(2,1)S(1)}, u32[]{:S(2)}, u32[]{:S(2)}) %collective-permute-start.13) | collective-permute-done | bytes 524320 | tf_op jit(solution)/shard_map/ppermute | solution.py:32
  170.9 1.1 collective-permute-start.9
  172.2 10.2 %collective-permute-done.9 = bf16[4,32,2048]{2,1,0:T(8,128)(2,1)S(1)} collective-permute-done((bf16[4,32,2048]{2,1,0:T(8,128)(2,1)S(1)}, bf16[4,32,2048]{2,1,0:T(8,128)(2,1)S(1)}, u32[]{:S(2)}, u32[]{:S(2)}) %collective-permute-start.9) | collective-permute-done | bytes 524320 | tf_op jit(solution)/shard_map/ppermute | solution.py:32
  182.9 7.1 %collective-permute-done.14 = bf16[2,32,2048]{2,1,0:T(8,128)(2,1)S(1)} collective-permute-done((bf16[2,32,2048]{2,1,0:T(8,128)(2,1)S(1)}, bf16[2,32,2048]{2,1,0:T(8,128)(2,1)S(1)}, u32[]{:S(2)}, u32[]{:S(2)}) %collective-permute-start.14) | collective-permute-done | bytes 262176 | tf_op jit(solution)/shard_map/ppermute | solution.py:32
  190.1 7.3 %collective-permute-done.10 = bf16[2,32,2048]{2,1,0:T(8,128)(2,1)S(1)} collective-permute-done((bf16[2,32,2048]{2,1,0:T(8,128)(2,1)S(1)}, bf16[2,32,2048]{2,1,0:T(8,128)(2,1)S(1)}, u32[]{:S(2)}, u32[]{:S(2)}) %collective-permute-start.10) | collective-permute-done | bytes 262176 | tf_op jit(solution)/shard_map/ppermute | solution.py:32
  197.7 8.8 %collective-permute-done.15 = bf16[1,32,2048]{2,1,0:T(8,128)(2,1)S(1)} collective-permute-done((bf16[1,32,2048]{2,1,0:T(8,128)(2,1)S(1)}, bf16[1,32,2048]{2,1,0:T(8,128)(2,1)S(1)}, u32[]{:S(2)}, u32[]{:S(2)}) %collective-permute-start.15) | collective-permute-done | bytes 131104 | tf_op jit(solution)/shard_map/ppermute | solution.py:32
  206.5 0.7 fusion.86
  207.9 0.7 all_to_all.8
  208.6 4.8 %all-to-all-start = ((f32[16,1,32]{2,1,0:T(1,128)}), f32[16,1,32]{2,1,0:T(1,128)S(1)}, u32[]{:S(2)}, u32[]{:S(2)}) async-start(f32[16,1,32]{2,1,0:T(1,128)} %bitcast.61), calls=%async_computation | async-start | bytes 16384 | tf_op jit(solution)/shard_map/all_to_all | solution.py:139
  213.4 0.7 fusion.85
  214.2 1.9 broadcast_select_fusion.2
  216.1 1.4 collective-permute-start.18
  217.5 2.0 broadcast_select_fusion.1
  220.7 0.8 slice.151
  221.8 2.8 %convolution_convert_fusion.2 = bf16[384,2048]{1,0:T(8,128)(2,1)S(1)} fusion(bf16[512,2176]{0,1:T(8,128)(2,1)} %collective-permute-done.16, s32[512]{0:T(512)S(1)} %convert_element_type.274, pred[512]{0:T(512)(128)(4,1)S(1)} %broadcast_compare_fusion), kind=kOutput, calls=%fused_computation.21 | convolution fusion | flops 806486016 | bytes 3672576 | tf_op jit(solution)/shard_map/dot_general | solution.py:11
  225.1 1.0 convolution_convert_fusion.3
  226.9 3.8 %fusion.33 = bf16[1,768,1024]{2,1,0:T(8,128)(2,1)} fusion(bf16[384,1024]{1,0:T(8,128)(2,1)S(1)} %multiply_convert_fusion.2, bf16[384,1024]{1,0:T(8,128)(2,1)S(1)} %multiply_convert_fusion.3, bf16[384,768]{1,0:T(8,128)(2,1)} %collective-permute-done.22, bf16[384,768]{1,0:T(8,128)(2,1)} %broadcast_select_fusion), kind=kOutput, calls=%fused_computation.49 | convolution fusion | flops 1214251008 | bytes 4325376 | tf_op jit(solution)/shard_map/dot_general | solution.py:11
  230.7 1.8 collective-permute-done.18
  232.5 3.8 %fusion.31 = bf16[1,1024,768]{2,1,0:T(8,128)(2,1)} fusion(bf16[384,768]{1,0:T(8,128)(2,1)} %collective-permute-done.18, bf16[384,768]{1,0:T(8,128)(2,1)} %broadcast_select_fusion.2, bf16[384,1024]{1,0:T(8,128)(2,1)S(1)} %slice.188, bf16[384,1024]{1,0:T(8,128)(2,1)S(1)} %slice.184), kind=kOutput, calls=%fused_computation.47 | convolution fusion | flops 1214251008 | bytes 4325376 | tf_op jit(solution)/shard_map/dot_general | solution.py:11
  236.4 8.3 %collective-permute-done.20 = bf16[384,768]{1,0:T(8,128)(2,1)} collective-permute-done((bf16[384,768]{1,0:T(8,128)(2,1)}, bf16[384,768]{1,0:T(8,128)(2,1)}, u32[]{:S(2)}, u32[]{:S(2)}) %collective-permute-start.20) | collective-permute-done | bytes 589856 | tf_op jit(solution)/shard_map/ppermute | solution.py:165
  244.7 4.0 %fusion.32 = bf16[1,1024,768]{2,1,0:T(8,128)(2,1)} fusion(bf16[384,768]{1,0:T(8,128)(2,1)} %collective-permute-done.20, bf16[384,768]{1,0:T(8,128)(2,1)} %broadcast_select_fusion.1, bf16[384,1024]{1,0:T(8,128)(2,1)S(1)} %slice.188, bf16[384,1024]{1,0:T(8,128)(2,1)S(1)} %slice.184), kind=kOutput, calls=%fused_computation.48 | convolution fusion | flops 1214251008 | bytes 4325376 | tf_op jit(solution)/shard_map/dot_general | solution.py:11
  (130 shorter events, 10.3 us)
Async XLA Ops:
  0.6 65.0 %copy-start = (bf16[1,768,2048]{2,1,0:T(8,128)(2,1)S(1)}, bf16[1,768,2048]{2,1,0:T(8,128)(2,1)}, u32[]{:S(2)}) copy-start(bf16[1,768,2048]{2,1,0:T(8,128)(2,1)} %param.13) | copy-start | bytes 9437188
  0.6 7.7 %collective-permute-start.4 = (bf16[32,2048]{1,0:T(8,128)(2,1)}, bf16[32,2048]{1,0:T(8,128)(2,1)S(1)}, u32[]{:S(2)}, u32[]{:S(2)}) collective-permute-start(bf16[32,2048]{1,0:T(8,128)(2,1)} %param.15), channel_id=1, source_target_pairs={{0,2},{1,3},{2,0},{3,1},{4,6},{5,7},{6,4},{7,5},{8,10},{9,11},{10,... | collective-permute-start | bytes 393224 | tf_op jit(solution)/shard_map/ppermute | solution.py:32
  5.7 9.2 %collective-permute-start = (bf16[32,2176]{1,0:T(8,128)(2,1)S(1)}, bf16[32,2176]{1,0:T(8,128)(2,1)S(1)}, u32[]{:S(2)}, u32[]{:S(2)}) collective-permute-start(bf16[32,2176]{1,0:T(8,128)(2,1)S(1)} %concatenate.24), channel_id=1, source_target_pairs={{0,8},{1,9},{2,10},{3,11},{4,12},{5,13},{6,14},{7,15},{8,0},{9,1},... | collective-permute-start | bytes 417800 | tf_op jit(solution)/shard_map/ppermute | solution.py:32
  9.3 10.9 %collective-permute-start.5 = (bf16[2,32,2048]{2,1,0:T(8,128)(2,1)S(1)}, bf16[2,32,2048]{2,1,0:T(8,128)(2,1)S(1)}, u32[]{:S(2)}, u32[]{:S(2)}) collective-permute-start(bf16[2,32,2048]{2,1,0:T(8,128)(2,1)S(1)} %pad_maximum_fusion.11), channel_id=1, source_target_pairs={{0,4},{1,5},{2,6},{3,7},{4,0},{5,1},{6,2},{7,3},{8,12},{9,13},{10,... | collective-permute-start | bytes 786440 | tf_op jit(solution)/shard_map/ppermute | solution.py:32
  14.9 14.1 %collective-permute-start.1 = (bf16[2,32,2176]{2,1,0:T(8,128)(2,1)S(1)}, bf16[2,32,2176]{2,1,0:T(8,128)(2,1)S(1)}, u32[]{:S(2)}, u32[]{:S(2)}) collective-permute-start(bf16[2,32,2176]{2,1,0:T(8,128)(2,1)S(1)} %pad_maximum_fusion.10), channel_id=1, source_target_pairs={{0,4},{1,5},{2,6},{3,7},{4,0},{5,1},{6,2},{7,3},{8,12},{9,13},{10,... | collective-permute-start | bytes 835592 | tf_op jit(solution)/shard_map/ppermute | solution.py:32
  20.3 23.2 %collective-permute-start.6 = (bf16[2,2,32,2048]{3,2,1,0:T(8,128)(2,1)S(1)}, bf16[2,2,32,2048]{3,2,1,0:T(8,128)(2,1)S(1)}, u32[]{:S(2)}, u32[]{:S(2)}) collective-permute-start(bf16[2,2,32,2048]{3,2,1,0:T(8,128)(2,1)S(1)} %pad_maximum_fusion.9), channel_id=1, source_target_pairs={{0,8},{1,9},{2,10},{3,11},{4,12},{5,13},{6,14},{7,15},{8,0},{9,1},... | collective-permute-start | bytes 1572872 | tf_op jit(solution)/shard_map/ppermute | solution.py:32
  29.1 15.7 %collective-permute-start.2 = (bf16[2,2,32,2176]{3,2,1,0:T(8,128)(2,1)S(1)}, bf16[2,2,32,2176]{3,2,1,0:T(8,128)(2,1)S(1)}, u32[]{:S(2)}, u32[]{:S(2)}) collective-permute-start(bf16[2,2,32,2176]{3,2,1,0:T(8,128)(2,1)S(1)} %pad_maximum_fusion.8), channel_id=1, source_target_pairs={{0,2},{1,3},{2,0},{3,1},{4,6},{5,7},{6,4},{7,5},{8,10},{9,11},{10,... | collective-permute-start | bytes 1671176 | tf_op jit(solution)/shard_map/ppermute | solution.py:32
  43.6 1.3 copy-start.12
  43.6 1.3 copy-start.13
  44.8 2.6 %copy-start.23 = (s32[16]{0:T(128)S(1)}, s32[16]{0:T(128)}, u32[]{:S(2)}) copy-start(s32[16]{0:T(128)} %param.14) | copy-start | bytes 196
  44.8 3.9 %collective-permute-start.7 = (bf16[2,2,2,32,2048]{4,3,2,1,0:T(8,128)(2,1)}, bf16[2,2,2,32,2048]{4,3,2,1,0:T(8,128)(2,1)}, u32[]{:S(2)}, u32[]{:S(2)}) collective-permute-start(bf16[2,2,2,32,2048]{4,3,2,1,0:T(8,128)(2,1)} %pad_maximum_fusion.5), channel_id=1, source_target_pairs={{0,1},{1,0},{2,3},{3,2},{4,5},{5,4},{6,7},{7,6},{8,9},{9,8},{10,11... | collective-permute-start | bytes 3145736 | tf_op jit(solution)/shard_map/ppermute | solution.py:32
  45.0 0.8 copy-start.8
  45.0 1.9 copy-start.10
  46.9 5.0 %collective-permute-start.3 = (bf16[2,2,2,32,2176]{4,3,2,1,0:T(8,128)(2,1)}, bf16[2,2,2,32,2176]{4,3,2,1,0:T(8,128)(2,1)}, u32[]{:S(2)}, u32[]{:S(2)}) collective-permute-start(bf16[2,2,2,32,2176]{4,3,2,1,0:T(8,128)(2,1)} %pad_maximum_fusion.4), channel_id=1, source_target_pairs={{0,1},{1,0},{2,3},{3,2},{4,5},{5,4},{6,7},{7,6},{8,9},{9,8},{10,11... | collective-permute-start | bytes 3342344 | tf_op jit(solution)/shard_map/ppermute | solution.py:32
  50.3 1.6 copy-start.9
  50.4 1.5 copy-start.11
  53.6 1.4 copy-start.2
  55.5 3.0 %copy-start.3 = (bf16[2,2,2,2,32,2176]{5,4,3,2,1,0:T(8,128)(2,1)S(1)}, bf16[2,2,2,2,32,2176]{5,4,3,2,1,0:T(8,128)(2,1)}, u32[]{:S(2)}) copy-start(bf16[2,2,2,2,32,2176]{5,4,3,2,1,0:T(8,128)(2,1)} %copy-done.2) | copy-start | bytes 6684676
  58.5 2.6 %copy-start.22 = (bf16[1,2048,768]{2,1,0:T(8,128)(2,1)S(1)}, bf16[1,2048,768]{2,1,0:T(8,128)(2,1)}, u32[]{:S(2)}) copy-start(bf16[1,2048,768]{2,1,0:T(8,128)(2,1)} %param.11) | copy-start | bytes 9437188
  61.1 1.9 copy-start.21
  63.0 1.6 copy-start.4
  65.6 3.0 %copy-start.14 = (bf16[384,2048]{1,0:T(8,128)(2,1)}, bf16[384,2048]{1,0:T(8,128)(2,1)S(1)}, u32[]{:S(2)}) copy-start(bf16[384,2048]{1,0:T(8,128)(2,1)S(1)} %convolution_convert_fusion.4) | copy-start | bytes 4718596
  72.8 144.7 %collective-permute-start.19 = (bf16[384,768]{1,0:T(8,128)(2,1)}, bf16[384,768]{1,0:T(8,128)(2,1)}, u32[]{:S(2)}, u32[]{:S(2)}) collective-permute-start(bf16[384,768]{1,0:T(8,128)(2,1)} %get-tuple-element.26), channel_id=1, source_target_pairs={{0,8},{1,9},{2,10},{3,11},{4,12},{5,13},{6,14},{7,15},{8,0},{9,1},... | collective-permute-start | bytes 1769480 | tf_op jit(solution)/shard_map/ppermute | solution.py:127
  72.8 141.4 %collective-permute-start.17 = (bf16[384,768]{1,0:T(8,128)(2,1)}, bf16[384,768]{1,0:T(8,128)(2,1)}, u32[]{:S(2)}, u32[]{:S(2)}) collective-permute-start(bf16[384,768]{1,0:T(8,128)(2,1)} %get-tuple-element.27), channel_id=1, source_target_pairs={{0,8},{1,9},{2,10},{3,11},{4,12},{5,13},{6,14},{7,15},{8,0},{9,1},... | collective-permute-start | bytes 1769480 | tf_op jit(solution)/shard_map/ppermute | solution.py:126
  75.7 76.7 %collective-permute-start.21 = (bf16[384,768]{1,0:T(8,128)(2,1)}, bf16[384,768]{1,0:T(8,128)(2,1)}, u32[]{:S(2)}, u32[]{:S(2)}) collective-permute-start(bf16[384,768]{1,0:T(8,128)(2,1)} %get-tuple-element.15), channel_id=1, source_target_pairs={{0,8},{1,9},{2,10},{3,11},{4,12},{5,13},{6,14},{7,15},{8,0},{9,1},... | collective-permute-start | bytes 1769480 | tf_op jit(solution)/shard_map/ppermute | solution.py:125
  78.2 1.1 copy-start.16
  81.0 10.3 %copy-start.5 = (bf16[512,2048]{1,0:T(8,128)(2,1)}, bf16[512,2048]{1,0:T(8,128)(2,1)S(1)}, u32[]{:S(2)}) copy-start(bf16[512,2048]{1,0:T(8,128)(2,1)S(1)} %convolution_convert_fusion.1) | copy-start | bytes 6291460
  91.3 64.6 %collective-permute-start.12 = (bf16[8,32,2048]{2,1,0:T(8,128)(2,1)}, bf16[8,32,2048]{2,1,0:T(8,128)(2,1)}, u32[]{:S(2)}, u32[]{:S(2)}) collective-permute-start(bf16[8,32,2048]{2,1,0:T(8,128)(2,1)} %select_bitcast_fusion.2), channel_id=1, source_target_pairs={{0,1},{1,0},{2,3},{3,2},{4,5},{5,4},{6,7},{7,6},{8,9},{9,8},{10,11... | collective-permute-start | bytes 3145736 | tf_op jit(solution)/shard_map/ppermute | solution.py:32
  92.4 65.9 %collective-permute-start.8 = (bf16[8,32,2048]{2,1,0:T(8,128)(2,1)}, bf16[8,32,2048]{2,1,0:T(8,128)(2,1)}, u32[]{:S(2)}, u32[]{:S(2)}) collective-permute-start(bf16[8,32,2048]{2,1,0:T(8,128)(2,1)} %select_bitcast_fusion.3), channel_id=1, source_target_pairs={{0,1},{1,0},{2,3},{3,2},{4,5},{5,4},{6,7},{7,6},{8,9},{9,8},{10,11... | collective-permute-start | bytes 3145736 | tf_op jit(solution)/shard_map/ppermute | solution.py:32
  103.0 53.4 %copy-start.7 = (bf16[512,2048]{1,0:T(8,128)(2,1)S(1)}, bf16[512,2048]{1,0:T(8,128)(2,1)}, u32[]{:S(2)}) copy-start(bf16[512,2048]{1,0:T(8,128)(2,1)} %convolution_convert_fusion) | copy-start | bytes 6291460
  152.4 68.3 %collective-permute-start.16 = (bf16[512,2176]{0,1:T(8,128)(2,1)}, bf16[512,2176]{0,1:T(8,128)(2,1)}, u32[]{:S(2)}, u32[]{:S(2)}) collective-permute-start(bf16[512,2176]{0,1:T(8,128)(2,1)} %pad_maximum_fusion.1), channel_id=1, source_target_pairs={{0,16},{16,0},{1,17},{17,1},{2,18},{18,2},{3,19},{19,3},{4,20},{20... | collective-permute-start | bytes 6684680 | tf_op jit(solution)/shard_map/ppermute | solution.py:164
  155.9 3.6 %copy-start.6 = (bf16[512,2048]{1,0:T(8,128)(2,1)S(1)}, bf16[512,2048]{1,0:T(8,128)(2,1)}, u32[]{:S(2)}) copy-start(bf16[512,2048]{1,0:T(8,128)(2,1)} %copy-done.5) | copy-start | bytes 6291460
  155.9 71.0 %collective-permute-start.22 = (bf16[384,768]{1,0:T(8,128)(2,1)}, bf16[384,768]{1,0:T(8,128)(2,1)}, u32[]{:S(2)}, u32[]{:S(2)}) collective-permute-start(bf16[384,768]{1,0:T(8,128)(2,1)} %broadcast_select_fusion), channel_id=1, source_target_pairs={{0,16},{16,0},{1,17},{17,1},{2,18},{18,2},{3,19},{19,3},{4,20},{20... | collective-permute-start | bytes 1769480 | tf_op jit(solution)/shard_map/ppermute | solution.py:165
  158.4 12.5 %collective-permute-start.13 = (bf16[4,32,2048]{2,1,0:T(8,128)(2,1)S(1)}, bf16[4,32,2048]{2,1,0:T(8,128)(2,1)S(1)}, u32[]{:S(2)}, u32[]{:S(2)}) collective-permute-start(bf16[4,32,2048]{2,1,0:T(8,128)(2,1)S(1)} %select_bitcast_fusion.8), channel_id=1, source_target_pairs={{0,2},{1,3},{2,0},{3,1},{4,6},{5,7},{6,4},{7,5},{8,10},{9,11},{10,... | collective-permute-start | bytes 1572872 | tf_op jit(solution)/shard_map/ppermute | solution.py:32
  170.9 11.6 %collective-permute-start.9 = (bf16[4,32,2048]{2,1,0:T(8,128)(2,1)S(1)}, bf16[4,32,2048]{2,1,0:T(8,128)(2,1)S(1)}, u32[]{:S(2)}, u32[]{:S(2)}) collective-permute-start(bf16[4,32,2048]{2,1,0:T(8,128)(2,1)S(1)} %fusion.63), channel_id=1, source_target_pairs={{0,2},{1,3},{2,0},{3,1},{4,6},{5,7},{6,4},{7,5},{8,10},{9,11},{10,... | collective-permute-start | bytes 1572872 | tf_op jit(solution)/shard_map/ppermute | solution.py:32
  182.5 7.5 %collective-permute-start.14 = (bf16[2,32,2048]{2,1,0:T(8,128)(2,1)S(1)}, bf16[2,32,2048]{2,1,0:T(8,128)(2,1)S(1)}, u32[]{:S(2)}, u32[]{:S(2)}) collective-permute-start(bf16[2,32,2048]{2,1,0:T(8,128)(2,1)S(1)} %select_bitcast_fusion.13), channel_id=1, source_target_pairs={{0,4},{1,5},{2,6},{3,7},{4,0},{5,1},{6,2},{7,3},{8,12},{9,13},{10,... | collective-permute-start | bytes 786440 | tf_op jit(solution)/shard_map/ppermute | solution.py:32
  182.8 24.4 %copy-start.15 = (bf16[384,2048]{1,0:T(8,128)(2,1)S(1)}, bf16[384,2048]{1,0:T(8,128)(2,1)}, u32[]{:S(2)}) copy-start(bf16[384,2048]{1,0:T(8,128)(2,1)} %copy-done.14) | copy-start | bytes 4718596
  182.8 24.4 %copy-start.17 = (bf16[384,2048]{1,0:T(8,128)(2,1)S(1)}, bf16[384,2048]{1,0:T(8,128)(2,1)}, u32[]{:S(2)}) copy-start(bf16[384,2048]{1,0:T(8,128)(2,1)} %copy-done.16) | copy-start | bytes 4718596
  190.0 7.5 %collective-permute-start.10 = (bf16[2,32,2048]{2,1,0:T(8,128)(2,1)S(1)}, bf16[2,32,2048]{2,1,0:T(8,128)(2,1)S(1)}, u32[]{:S(2)}, u32[]{:S(2)}) collective-permute-start(bf16[2,32,2048]{2,1,0:T(8,128)(2,1)S(1)} %fusion.79), channel_id=1, source_target_pairs={{0,4},{1,5},{2,6},{3,7},{4,0},{5,1},{6,2},{7,3},{8,12},{9,13},{10,... | collective-permute-start | bytes 786440 | tf_op jit(solution)/shard_map/ppermute | solution.py:32
  197.4 9.1 %collective-permute-start.15 = (bf16[1,32,2048]{2,1,0:T(8,128)(2,1)S(1)}, bf16[1,32,2048]{2,1,0:T(8,128)(2,1)S(1)}, u32[]{:S(2)}, u32[]{:S(2)}) collective-permute-start(bf16[1,32,2048]{2,1,0:T(8,128)(2,1)S(1)} %select_bitcast_fusion.18), channel_id=1, source_target_pairs={{0,8},{1,9},{2,10},{3,11},{4,12},{5,13},{6,14},{7,15},{8,0},{9,1},... | collective-permute-start | bytes 393224 | tf_op jit(solution)/shard_map/ppermute | solution.py:32
  206.5 6.9 %collective-permute-start.11 = (bf16[1,32,2048]{2,1,0:T(8,128)(2,1)S(1)}, bf16[1,32,2048]{2,1,0:T(8,128)(2,1)S(1)}, u32[]{:S(2)}, u32[]{:S(2)}) collective-permute-start(bf16[1,32,2048]{2,1,0:T(8,128)(2,1)S(1)} %select_bitcast_fusion.19), channel_id=1, source_target_pairs={{0,8},{1,9},{2,10},{3,11},{4,12},{5,13},{6,14},{7,15},{8,0},{9,1},... | collective-permute-start | bytes 393224 | tf_op jit(solution)/shard_map/ppermute | solution.py:32
  207.7 12.4 %copy-start.20 = (s32[32,8]{0,1:T(8,128)S(1)}, s32[32,8]{0,1:T(8,128)}, u32[]{:S(2)}) copy-start(s32[32,8]{0,1:T(8,128)} %param.9) | copy-start | bytes 3076
  208.6 11.5 %all-to-all-start = ((f32[16,1,32]{2,1,0:T(1,128)}), f32[16,1,32]{2,1,0:T(1,128)S(1)}, u32[]{:S(2)}, u32[]{:S(2)}) async-start(f32[16,1,32]{2,1,0:T(1,128)} %bitcast.61), calls=%async_computation | async-start | bytes 16384 | tf_op jit(solution)/shard_map/all_to_all | solution.py:139
  216.1 16.4 %collective-permute-start.18 = (bf16[384,768]{1,0:T(8,128)(2,1)}, bf16[384,768]{1,0:T(8,128)(2,1)}, u32[]{:S(2)}, u32[]{:S(2)}) collective-permute-start(bf16[384,768]{1,0:T(8,128)(2,1)} %broadcast_select_fusion.2), channel_id=1, source_target_pairs={{0,16},{16,0},{1,17},{17,1},{2,18},{18,2},{3,19},{19,3},{4,20},{20... | collective-permute-start | bytes 1769480 | tf_op jit(solution)/shard_map/ppermute | solution.py:165
  219.5 25.2 %collective-permute-start.20 = (bf16[384,768]{1,0:T(8,128)(2,1)}, bf16[384,768]{1,0:T(8,128)(2,1)}, u32[]{:S(2)}, u32[]{:S(2)}) collective-permute-start(bf16[384,768]{1,0:T(8,128)(2,1)} %broadcast_select_fusion.1), channel_id=1, source_target_pairs={{0,16},{16,0},{1,17},{17,1},{2,18},{18,2},{3,19},{19,3},{4,20},{20... | collective-permute-start | bytes 1769480 | tf_op jit(solution)/shard_map/ppermute | solution.py:165
  221.8 3.3 %copy-start.18 = (bf16[512,1024]{0,1:T(8,128)(2,1)S(1)}, bf16[512,1024]{0,1:T(8,128)(2,1)}, u32[]{:S(2)}) copy-start(bf16[512,1024]{0,1:T(8,128)(2,1)} %get-tuple-element.33) | copy-start | bytes 3145732
  221.8 3.3 %copy-start.19 = (bf16[512,1024]{0,1:T(8,128)(2,1)S(1)}, bf16[512,1024]{0,1:T(8,128)(2,1)}, u32[]{:S(2)}) copy-start(bf16[512,1024]{0,1:T(8,128)(2,1)} %get-tuple-element.53) | copy-start | bytes 3145732
  244.7 4.0 %copy-start.1 = (bf16[1,768,2048]{2,1,0:T(8,128)(2,1)S(1)}, bf16[1,768,2048]{2,1,0:T(8,128)(2,1)}, u32[]{:S(2)}) copy-start(bf16[1,768,2048]{2,1,0:T(8,128)(2,1)} %param.13) | copy-start | bytes 9437188

commit v4 on v3

--- a/solution.py
+++ b/solution.py
@@ -123,8 +123,8 @@
     trade = [(i, (i + half) % experts) for i in range(experts)]
 
     far_hidden = lax.ppermute(hidden, "expert", trade)
-    far_gate = lax.ppermute(d_gate_pre, "expert", trade)
-    far_up = lax.ppermute(d_up_pre, "expert", trade)
+    pres = jnp.concatenate([d_gate_pre, d_up_pre], axis=1)
+    far_pres = lax.ppermute(pres, "expert", trade)
 
     result = dot(after(hidden, d_gate_pre, d_up_pre), down_mat, 1, 0).astype(BF16)
     result_f = result.astype(F32)
@@ -143,9 +143,8 @@
 
     placed = jnp.where(swapped, (own + half) % experts, own)
     acts = (
-        jnp.where(swapped, after(far_hidden, d_spread), hidden),
-        jnp.where(swapped, after(far_gate, mixture), d_gate_pre),
-        jnp.where(swapped, after(far_up, d_tokens), d_up_pre),
+        jnp.where(swapped, after(far_hidden, mixture, d_tokens), hidden),
+        jnp.where(swapped, after(far_pres, mixture, d_tokens), pres),
     )
     late_tokens, late_d_out, late_table = lax.optimization_barrier(
         (tokens_all, d_out_all, table, d_gate_pre, d_up_pre)
@@ -161,7 +160,7 @@
         parts = acts
         if shift:
             ring = [(i, (i + shift) % groups) for i in range(groups)]
-            block = after(lax.ppermute(block, "dp", ring), mixture)
+            block = after(lax.ppermute(block, "dp", ring), mixture, d_tokens)
             parts = [lax.ppermute(a, "dp", ring) for a in acts]
         choose, scale = row_picker(column_of(block[:, 2 * part :], placed), capacity)
         chosen = dot(choose, block[:, : 2 * part], 1, 0).astype(BF16)
@@ -169,11 +168,11 @@
         cots.append((scale * chosen[:, part:].astype(F32)).astype(BF16))
         acts_of.append(parts)
     x, cot = jnp.concatenate(xs), jnp.concatenate(cots)
-    hidden, d_gate_pre, d_up_pre = (jnp.concatenate(a) for a in zip(*acts_of))
+    hidden, pres = (jnp.concatenate(a) for a in zip(*acts_of))
     g_down = dot(hidden, cot, 0, 0).astype(BF16)
-    g_gate = dot(x, d_gate_pre, 0, 0).astype(BF16)
-    g_up = dot(x, d_up_pre, 0, 0).astype(BF16)
-    return (mixture, d_tokens, d_gates, g_gate[None], g_up[None], g_down[None])
+    g_pre = dot(x, pres, 0, 0).astype(BF16)
+    ff = hidden.shape[1]
+    return (mixture, d_tokens, d_gates, g_pre[None, :, :ff], g_pre[None, :, ff:], g_down[None])
 
 
 def solution(mesh):

time: 250 us -> 222 us (0.89)
  waiting for transfers between devices: 131 us -> 94.9 us
  starting transfers between devices: 25.1 us -> 35.4 us
  local copies, waits for them, and re-layouts: 20.3 us -> 24.3 us
  matrix products: 41.4 us -> 37.7 us
    ppermute x1, waiting for transfers between devices: 47.9 us -> 0.01 us  [on_device(): far_hidden = lax.ppermute(hidden, 'expert', trade)]
    ppermute x16, starting transfers between devices: 13.2 us -> 23.3 us  [swap_bit(): lax.ppermute(value, 'expert', [(i, i ^ 1 << bit) for i in range(size)])]
    ppermute x16, waiting for transfers between devices: 72.8 us -> 79.9 us  [swap_bit(): lax.ppermute(value, 'expert', [(i, i ^ 1 << bit) for i in range(size)])]
    dot_general x17 -> x16, matrix products: 41.4 us -> 37.7 us  [dot(): lax.dot_general(left, right, (((lhs_dim,), (rhs_dim,)), ((), ())), prefer...]
    all_to_all x1, waiting for transfers between devices: 0.01 us -> 3.16 us  [on_device(): lax.all_to_all(inner, 'expert', split_axis=0, concat_axis=0, tiled=True)]
    select_n x3 -> x2, other arithmetic: 5.88 us -> 3.57 us  [the longest x1 2.02 us: on_device(): jnp.where(swapped, after(far_hidden, mixture, d_tokens), hidden)]
    unnamed x50 -> x66, local copies, waits for them, and re-layouts: 6.8 us -> 8.92 us
    ppermute x3 -> x2, waiting for transfers between devices: 10.1 us -> 11.8 us  [on_device(): parts = [lax.ppermute(a, 'dp', ring) for a in acts]]
  transfers between devices with their start and end apart: 24 -> 22, of which waited for: 12 -> 11; matrix products, arithmetic and copies ran while one was open for 25% -> 27% of each run, Pallas kernels for 0% -> 0%
where the time goes in v4:
time: 222 us; the launch traced here: 221 us
  waiting for transfers between devices  94.9 us (43%)
  matrix products  37.7 us (17%)
  starting transfers between devices  35.4 us (16%)
  other arithmetic  26.7 us (12%)
  local copies, waits for them, and re-layouts  24.3 us (11%)
    ppermute x16, waiting for transfers between devices, swap_bit(): lax.ppermute(value, 'expert', [(i, i ^ 1 << bit) for i in range(size)])  79.9 us
    dot_general x16, matrix products, dot(): lax.dot_general(left, right, (((lhs_dim,), (rhs_dim,)), ((), ())), prefer...  37.7 us
    ppermute x16, starting transfers between devices, swap_bit(): lax.ppermute(value, 'expert', [(i, i ^ 1 << bit) for i in range(size)])  23.3 us
    ppermute x2, waiting for transfers between devices, on_device(): parts = [lax.ppermute(a, 'dp', ring) for a in acts]  11.8 us
    unnamed x66, local copies, waits for them, and re-layouts  8.92 us
    another operation x16, other arithmetic, gather_rows(): jnp.stack([jnp.where(high, other, held), jnp.where(high, held, other)], a...  8.61 us
    optimization_barrier x3, local copies, waits for them, and re-layouts, on_device(): lax.optimization_barrier((tokens_all, d_out_all, table, d_gate_pre, d_up_...  6.91 us
    all_to_all x1, starting transfers between devices, on_device(): lax.all_to_all(inner, 'expert', split_axis=0, concat_axis=0, tiled=True)  4.73 us
  transfers between devices with their start and end apart: 22, of which 11 were waited for; matrix products, arithmetic and copies ran while one was open for 27% of the time, Pallas kernels for 0%

profile of v4, /device:TPU:0, one launch (start us, length us, event | category | flops | bytes accessed | tf_op | source)
XLA Modules:
  0.0 220.9 jit_solution(2702365817424692689)
XLA Ops:
  0.6 3.0 %collective-permute-start.4 = (bf16[32,2048]{1,0:T(8,128)(2,1)}, bf16[32,2048]{1,0:T(8,128)(2,1)S(1)}, u32[]{:S(2)}, u32[]{:S(2)}) collective-permute-start(bf16[32,2048]{1,0:T(8,128)(2,1)} %param.15), channel_id=1, source_target_pairs={{0,2},{1,3},{2,0},{3,1},{4,6},{5,7},{6,4},{7,5},{8,10},{9,11},{10,... | collective-permute-start | bytes 393224 | tf_op jit(solution)/shard_map/ppermute | solution.py:32
  4.7 1.0 concatenate.24
  5.7 2.6 %collective-permute-start = (bf16[32,2176]{1,0:T(8,128)(2,1)S(1)}, bf16[32,2176]{1,0:T(8,128)(2,1)S(1)}, u32[]{:S(2)}, u32[]{:S(2)}) collective-permute-start(bf16[32,2176]{1,0:T(8,128)(2,1)S(1)} %concatenate.24), channel_id=1, source_target_pairs={{0,8},{1,9},{2,10},{3,11},{4,12},{5,13},{6,14},{7,15},{8,0},{9,1},... | collective-permute-start | bytes 417800 | tf_op jit(solution)/shard_map/ppermute | solution.py:32
  8.3 0.9 select_bitcast_fusion.21
  9.3 1.6 collective-permute-start.5
  10.9 3.9 %collective-permute-done = bf16[32,2176]{1,0:T(8,128)(2,1)S(1)} collective-permute-done((bf16[32,2176]{1,0:T(8,128)(2,1)S(1)}, bf16[32,2176]{1,0:T(8,128)(2,1)S(1)}, u32[]{:S(2)}, u32[]{:S(2)}) %collective-permute-start) | collective-permute-done | bytes 139296 | tf_op jit(solution)/shard_map/ppermute | solution.py:32
  15.6 4.6 %collective-permute-done.5 = bf16[2,32,2048]{2,1,0:T(8,128)(2,1)S(1)} collective-permute-done((bf16[2,32,2048]{2,1,0:T(8,128)(2,1)S(1)}, bf16[2,32,2048]{2,1,0:T(8,128)(2,1)S(1)}, u32[]{:S(2)}, u32[]{:S(2)}) %collective-permute-start.5) | collective-permute-done | bytes 262176 | tf_op jit(solution)/shard_map/ppermute | solution.py:32
  20.3 1.5 collective-permute-start.6
  21.8 7.2 %collective-permute-done.1 = bf16[2,32,2176]{2,1,0:T(8,128)(2,1)S(1)} collective-permute-done((bf16[2,32,2176]{2,1,0:T(8,128)(2,1)S(1)}, bf16[2,32,2176]{2,1,0:T(8,128)(2,1)S(1)}, u32[]{:S(2)}, u32[]{:S(2)}) %collective-permute-start.1) | collective-permute-done | bytes 278560 | tf_op jit(solution)/shard_map/ppermute | solution.py:32
  29.4 14.1 %collective-permute-done.6 = bf16[2,2,32,2048]{3,2,1,0:T(8,128)(2,1)S(1)} collective-permute-done((bf16[2,2,32,2048]{3,2,1,0:T(8,128)(2,1)S(1)}, bf16[2,2,32,2048]{3,2,1,0:T(8,128)(2,1)S(1)}, u32[]{:S(2)}, u32[]{:S(2)}) %collective-permute-start.6) | collective-permute-done | bytes 524320 | tf_op jit(solution)/shard_map/ppermute | solution.py:32
  43.6 1.2 pad_maximum_fusion.5
  45.0 0.8 copy-done.8
  45.8 1.1 pad_maximum_fusion.4
  48.7 1.7 select_bitcast_fusion.5
  50.4 1.5 pad_maximum_fusion.2
  51.9 1.5 select_bitcast_fusion.1
  53.7 1.4 copy-done.2
  55.7 2.7 %convolution_convert_fusion.6 = bf16[384,2048]{1,0:T(8,128)(2,1)S(1)} fusion(s32[512]{0:T(512)S(1)} %convert_element_type.220, pred[512]{0:T(512)(128)(4,1)S(1)} %broadcast_compare_fusion.2, bf16[512,2176]{1,0:T(8,128)(2,1)} %bitcast.247), kind=kOutput, calls=%fused_computation.25 | convolution fusion | flops 806486016 | bytes 3672576 | tf_op jit(solution)/shard_map/dot_general | solution.py:11
  58.5 1.0 convolution_convert_fusion.5
  59.5 0.9 copy-done.30
  60.4 1.4 fusion.12
  61.8 1.1 copy-done.29
  62.8 1.4 fusion.8
  64.3 2.8 %multiply_convert_fusion.4 = (bf16[384,768]{1,0:T(8,128)(2,1)S(1)}, bf16[384,768]{1,0:T(8,128)(2,1)}, bf16[384,768]{1,0:T(8,128)(2,1)}) fusion(f32[384,768]{1,0:T(8,128)S(1)} %fusion.12, f32[384,768]{1,0:T(8,128)S(1)} %fusion.8, bf16[1,768,2048]{2,1,0:T(8,128)(2,1)S(1)} %copy-done, bf16[384,2048]{1,0:T(8,128)(2,1)S(1)} %convolution_convert_fusion.5, ...), kind=kOutput, calls=%fused_computation.58 | convolution fusion | flops 1214742528 | bytes 8848896 | tf_op jit(solution)/shard_map/dot_general | solution.py:11
  67.0 3.1 %fusion.6 = f32[384,2048]{1,0:T(8,128)} fusion(bf16[384,768]{1,0:T(8,128)(2,1)S(1)} %get-tuple-element.26, bf16[1,2048,768]{2,1,0:T(8,128)(2,1)S(1)} %copy-done.29), kind=kOutput, calls=%fused_computation.9 | convolution fusion | flops 1207959552 | bytes 6881280 | tf_op jit(solution)/shard_map/dot_general | solution.py:11
  70.1 6.9 %convolution_convert_fusion.1 = bf16[512,2048]{1,0:T(8,128)(2,1)} fusion(f32[384,2048]{1,0:T(8,128)} %fusion.6, bf16[384,768]{1,0:T(8,128)(2,1)} %get-tuple-element.27, bf16[1,2048,768]{2,1,0:T(8,128)(2,1)} %param.11, s32[512]{0:T(512)S(1)} %convert_element_type.220, pred[512]{0:T(512)(128)(4,1)S(1)} %broadcast_compare_fusion.2), kind=kOutput, calls=%fused_computation.19 | convolution fusion | flops 2016280576 | bytes 8980992 | tf_op jit(solution)/shard_map/dot_general | solution.py:11
  77.0 2.6 %select_bitcast_fusion.2 = bf16[8,32,2048]{2,1,0:T(8,128)(2,1)} fusion(pred[]{:T(512)S(6)} %eq.126, bf16[8,2,32,2048]{3,2,1,0:T(8,128)(2,1)} %bitcast.258), kind=kLoop, calls=%fused_computation.76 | loop fusion | flops 524288 | bytes 3145729 | tf_op jit(solution)/shard_map/jit(_where)/select_n | solution.py:56
  79.7 2.4 %fusion.16 = bf16[384,2048]{1,0:T(8,128)(2,1)S(1)} fusion(bf16[384,768]{1,0:T(8,128)(2,1)} %get-tuple-element.14, bf16[1,768,2048]{2,1,0:T(8,128)(2,1)S(1)} %copy-done), kind=kOutput, calls=%fused_computation.21 | convolution fusion | flops 1208745984 | bytes 5308416 | tf_op jit(solution)/shard_map/dot_general | solution.py:11
  82.2 1.4 convolution_convert_fusion.2
  83.6 1.4 copy-done.5
  85.0 1.1 select_bitcast_fusion.3
  86.1 1.6 slice.171
  88.3 2.9 %copy.160 = bf16[512,2048]{0,1:T(8,128)(2,1)S(1)} copy(bf16[512,2048]{1,0:T(8,128)(2,1)} %slice.171) | data formatting | bytes 4194304 | tf_op jit(solution)/shard_map/optimization_barrier | solution.py:149
  91.3 3.9 %copy.157 = bf16[512,2048]{0,1:T(8,128)(2,1)} copy(bf16[512,2048]{1,0:T(8,128)(2,1)} %bitcast.254) | data formatting | bytes 4194304 | tf_op jit(solution)/shard_map/optimization_barrier | solution.py:149
  95.2 3.2 %constant_dynamic-slice_fusion.2 = (bf16[512,1024]{0,1:T(8,128)(2,1)}, bf16[512,1024]{0,1:T(8,128)(2,1)S(1)}, bf16[512,1024]{0,1:T(8,128)(2,1)S(1)}, bf16[512,1024]{0,1:T(8,128)(2,1)}) fusion(bf16[512,2048]{0,1:T(8,128)(2,1)} %copy.157, s32[]{:T(128)S(6)} %select_n.442, s32[]{:T(128)S(6)} %select_n.444, bf16[512,2048]{0,1:T(8,128)(2,1)S(1)} %copy.160), kind=kLoop, calls=%fused_computation.181 | loop fusion | bytes 8388616 | tf_op jit(solution)/shard_map/dynamic_slice | solution.py:156
  98.4 1.5 pad_maximum_fusion.1
  100.2 1.6 collective-permute-start.16
  101.8 3.0 %collective-permute-start.17 = (bf16[384,1536]{1,0:T(8,128)(2,1)S(1)}, bf16[384,1536]{1,0:T(8,128)(2,1)S(1)}, u32[]{:S(2)}, u32[]{:S(2)}) collective-permute-start(bf16[384,1536]{1,0:T(8,128)(2,1)S(1)} %pad_maximum_fusion.3), channel_id=1, source_target_pairs={{0,8},{1,9},{2,10},{3,11},{4,12},{5,13},{6,14},{7,15},{8,0},{9,1},... | collective-permute-start | bytes 3538952 | tf_op jit(solution)/shard_map/ppermute | solution.py:127
  104.8 1.7 fusion.25
  106.6 1.1 collective-permute-start.13
  107.8 1.7 fusion.26
  109.6 1.0 collective-permute-start.9
  110.6 10.9 %collective-permute-done.13 = bf16[4,32,2048]{2,1,0:T(8,128)(2,1)S(1)} collective-permute-done((bf16[4,32,2048]{2,1,0:T(8,128)(2,1)S(1)}, bf16[4,32,2048]{2,1,0:T(8,128)(2,1)S(1)}, u32[]{:S(2)}, u32[]{:S(2)}) %collective-permute-start.13) | collective-permute-done | bytes 524320 | tf_op jit(solution)/shard_map/ppermute | solution.py:32
  121.8 1.3 collective-permute-start.14
  123.2 8.0 %collective-permute-done.9 = bf16[4,32,2048]{2,1,0:T(8,128)(2,1)S(1)} collective-permute-done((bf16[4,32,2048]{2,1,0:T(8,128)(2,1)S(1)}, bf16[4,32,2048]{2,1,0:T(8,128)(2,1)S(1)}, u32[]{:S(2)}, u32[]{:S(2)}) %collective-permute-start.9) | collective-permute-done | bytes 524320 | tf_op jit(solution)/shard_map/ppermute | solution.py:32
  131.5 2.0 collective-permute-start.10
  133.5 3.3 %collective-permute-done.14 = bf16[2,32,2048]{2,1,0:T(8,128)(2,1)S(1)} collective-permute-done((bf16[2,32,2048]{2,1,0:T(8,128)(2,1)S(1)}, bf16[2,32,2048]{2,1,0:T(8,128)(2,1)S(1)}, u32[]{:S(2)}, u32[]{:S(2)}) %collective-permute-start.14) | collective-permute-done | bytes 262176 | tf_op jit(solution)/shard_map/ppermute | solution.py:32
  137.0 4.6 %collective-permute-start.15 = (bf16[1,32,2048]{2,1,0:T(8,128)(2,1)S(1)}, bf16[1,32,2048]{2,1,0:T(8,128)(2,1)S(1)}, u32[]{:S(2)}, u32[]{:S(2)}) collective-permute-start(bf16[1,32,2048]{2,1,0:T(8,128)(2,1)S(1)} %select_bitcast_fusion.18), channel_id=1, source_target_pairs={{0,8},{1,9},{2,10},{3,11},{4,12},{5,13},{6,14},{7,15},{8,0},{9,1},... | collective-permute-start | bytes 393224 | tf_op jit(solution)/shard_map/ppermute | solution.py:32
  141.6 22.1 %collective-permute-done.10 = bf16[2,32,2048]{2,1,0:T(8,128)(2,1)S(1)} collective-permute-done((bf16[2,32,2048]{2,1,0:T(8,128)(2,1)S(1)}, bf16[2,32,2048]{2,1,0:T(8,128)(2,1)S(1)}, u32[]{:S(2)}, u32[]{:S(2)}) %collective-permute-start.10) | collective-permute-done | bytes 262176 | tf_op jit(solution)/shard_map/ppermute | solution.py:32
  163.8 2.4 %collective-permute-start.11 = (bf16[1,32,2048]{2,1,0:T(8,128)(2,1)S(1)}, bf16[1,32,2048]{2,1,0:T(8,128)(2,1)S(1)}, u32[]{:S(2)}, u32[]{:S(2)}) collective-permute-start(bf16[1,32,2048]{2,1,0:T(8,128)(2,1)S(1)} %select_bitcast_fusion.19), channel_id=1, source_target_pairs={{0,8},{1,9},{2,10},{3,11},{4,12},{5,13},{6,14},{7,15},{8,0},{9,1},... | collective-permute-start | bytes 393224 | tf_op jit(solution)/shard_map/ppermute | solution.py:32
  166.9 5.8 %collective-permute-done.11 = bf16[1,32,2048]{2,1,0:T(8,128)(2,1)S(1)} collective-permute-done((bf16[1,32,2048]{2,1,0:T(8,128)(2,1)S(1)}, bf16[1,32,2048]{2,1,0:T(8,128)(2,1)S(1)}, u32[]{:S(2)}, u32[]{:S(2)}) %collective-permute-start.11) | collective-permute-done | bytes 131104 | tf_op jit(solution)/shard_map/ppermute | solution.py:32
  173.4 2.0 broadcast_select_fusion.1
  175.4 1.2 collective-permute-start.20
  178.5 4.7 %all-to-all-start = ((f32[16,1,32]{2,1,0:T(1,128)}), f32[16,1,32]{2,1,0:T(1,128)S(1)}, u32[]{:S(2)}, u32[]{:S(2)}) async-start(f32[16,1,32]{2,1,0:T(1,128)} %bitcast.61), calls=%async_computation | async-start | bytes 16384 | tf_op jit(solution)/shard_map/all_to_all | solution.py:139
  183.3 1.5 broadcast_select_fusion
  184.8 1.6 collective-permute-start.18
  186.4 3.2 %all-to-all-done = f32[16,1,32]{2,1,0:T(1,128)S(1)} async-done(((f32[16,1,32]{2,1,0:T(1,128)}), f32[16,1,32]{2,1,0:T(1,128)S(1)}, u32[]{:S(2)}, u32[]{:S(2)}) %all-to-all-start) | async-done | bytes 2080 | tf_op jit(solution)/shard_map/all_to_all | solution.py:139
  190.2 0.8 slice.157
  191.8 2.6 %convolution_convert_fusion.4 = bf16[384,2048]{1,0:T(8,128)(2,1)S(1)} fusion(bf16[512,1024]{0,1:T(8,128)(2,1)} %get-tuple-element.33, bf16[512,1024]{0,1:T(8,128)(2,1)} %get-tuple-element.53, s32[512]{0:T(512)S(1)} %convert_element_type.269, pred[512]{0:T(512)(128)(4,1)S(1)} %broadcast_compare_fusion.1), kind=kOutput, calls=%fused_computation.23 | convolution fusion | flops 810680320 | bytes 3672576 | tf_op jit(solution)/shard_map/dot_general | solution.py:11
  194.4 3.2 %convolution_convert_fusion.3 = bf16[384,2048]{1,0:T(8,128)(2,1)S(1)} fusion(bf16[512,2176]{0,1:T(8,128)(2,1)} %collective-permute-done.16, s32[512]{0:T(512)S(1)} %convert_element_type.271, pred[512]{0:T(512)(128)(4,1)S(1)} %broadcast_compare_fusion), kind=kOutput, calls=%fused_computation.22 | convolution fusion | flops 806486016 | bytes 3672576 | tf_op jit(solution)/shard_map/dot_general | solution.py:11
  198.9 4.0 %fusion.37 = bf16[1,768,1024]{2,1,0:T(8,128)(2,1)} fusion(bf16[384,1024]{1,0:T(8,128)(2,1)S(1)} %multiply_convert_fusion.2, bf16[384,1024]{1,0:T(8,128)(2,1)S(1)} %multiply_convert_fusion.3, bf16[384,768]{1,0:T(8,128)(2,1)} %collective-permute-done.20, bf16[384,768]{1,0:T(8,128)(2,1)} %broadcast_select_fusion.1), kind=kOutput, calls=%fused_computation.53 | convolution fusion | flops 1214251008 | bytes 4325376 | tf_op jit(solution)/shard_map/dot_general | solution.py:11
  202.9 11.8 %collective-permute-done.18 = bf16[384,1536]{1,0:T(8,128)(2,1)} collective-permute-done((bf16[384,1536]{1,0:T(8,128)(2,1)S(1)}, bf16[384,1536]{1,0:T(8,128)(2,1)}, u32[]{:S(2)}, u32[]{:S(2)}) %collective-permute-start.18) | collective-permute-done | bytes 1179680 | tf_op jit(solution)/shard_map/ppermute | solution.py:164
  214.7 4.3 %convolution_convert_fusion = bf16[1024,1536]{1,0:T(8,128)(2,1)S(1)} fusion(bf16[384,1536]{1,0:T(8,128)(2,1)} %collective-permute-done.18, bf16[384,1536]{1,0:T(8,128)(2,1)S(1)} %copy-done.27, bf16[384,1024]{1,0:T(8,128)(2,1)S(1)} %slice-done.1, bf16[384,1024]{1,0:T(8,128)(2,1)S(1)} %slice-done), kind=kOutput, calls=%fused_computation.2 | convolution fusion | flops 2425356288 | bytes 7077888 | tf_op jit(solution)/shard_map/dot_general | solution.py:11
  219.1 1.9 slice_bitcast_fusion
  (144 shorter events, 12.5 us)
Async XLA Ops:
  0.6 63.6 %copy-start = (bf16[1,768,2048]{2,1,0:T(8,128)(2,1)S(1)}, bf16[1,768,2048]{2,1,0:T(8,128)(2,1)}, u32[]{:S(2)}) copy-start(bf16[1,768,2048]{2,1,0:T(8,128)(2,1)} %param.13) | copy-start | bytes 9437188
  0.6 7.7 %collective-permute-start.4 = (bf16[32,2048]{1,0:T(8,128)(2,1)}, bf16[32,2048]{1,0:T(8,128)(2,1)S(1)}, u32[]{:S(2)}, u32[]{:S(2)}) collective-permute-start(bf16[32,2048]{1,0:T(8,128)(2,1)} %param.15), channel_id=1, source_target_pairs={{0,2},{1,3},{2,0},{3,1},{4,6},{5,7},{6,4},{7,5},{8,10},{9,11},{10,... | collective-permute-start | bytes 393224 | tf_op jit(solution)/shard_map/ppermute | solution.py:32
  5.7 9.2 %collective-permute-start = (bf16[32,2176]{1,0:T(8,128)(2,1)S(1)}, bf16[32,2176]{1,0:T(8,128)(2,1)S(1)}, u32[]{:S(2)}, u32[]{:S(2)}) collective-permute-start(bf16[32,2176]{1,0:T(8,128)(2,1)S(1)} %concatenate.24), channel_id=1, source_target_pairs={{0,8},{1,9},{2,10},{3,11},{4,12},{5,13},{6,14},{7,15},{8,0},{9,1},... | collective-permute-start | bytes 417800 | tf_op jit(solution)/shard_map/ppermute | solution.py:32
  9.3 10.9 %collective-permute-start.5 = (bf16[2,32,2048]{2,1,0:T(8,128)(2,1)S(1)}, bf16[2,32,2048]{2,1,0:T(8,128)(2,1)S(1)}, u32[]{:S(2)}, u32[]{:S(2)}) collective-permute-start(bf16[2,32,2048]{2,1,0:T(8,128)(2,1)S(1)} %pad_maximum_fusion.9), channel_id=1, source_target_pairs={{0,4},{1,5},{2,6},{3,7},{4,0},{5,1},{6,2},{7,3},{8,12},{9,13},{10,... | collective-permute-start | bytes 786440 | tf_op jit(solution)/shard_map/ppermute | solution.py:32
  14.9 14.1 %collective-permute-start.1 = (bf16[2,32,2176]{2,1,0:T(8,128)(2,1)S(1)}, bf16[2,32,2176]{2,1,0:T(8,128)(2,1)S(1)}, u32[]{:S(2)}, u32[]{:S(2)}) collective-permute-start(bf16[2,32,2176]{2,1,0:T(8,128)(2,1)S(1)} %pad_maximum_fusion.8), channel_id=1, source_target_pairs={{0,4},{1,5},{2,6},{3,7},{4,0},{5,1},{6,2},{7,3},{8,12},{9,13},{10,... | collective-permute-start | bytes 835592 | tf_op jit(solution)/shard_map/ppermute | solution.py:32
  20.3 23.2 %collective-permute-start.6 = (bf16[2,2,32,2048]{3,2,1,0:T(8,128)(2,1)S(1)}, bf16[2,2,32,2048]{3,2,1,0:T(8,128)(2,1)S(1)}, u32[]{:S(2)}, u32[]{:S(2)}) collective-permute-start(bf16[2,2,32,2048]{3,2,1,0:T(8,128)(2,1)S(1)} %pad_maximum_fusion.7), channel_id=1, source_target_pairs={{0,8},{1,9},{2,10},{3,11},{4,12},{5,13},{6,14},{7,15},{8,0},{9,1},... | collective-permute-start | bytes 1572872 | tf_op jit(solution)/shard_map/ppermute | solution.py:32
  29.1 15.7 %collective-permute-start.2 = (bf16[2,2,32,2176]{3,2,1,0:T(8,128)(2,1)S(1)}, bf16[2,2,32,2176]{3,2,1,0:T(8,128)(2,1)S(1)}, u32[]{:S(2)}, u32[]{:S(2)}) collective-permute-start(bf16[2,2,32,2176]{3,2,1,0:T(8,128)(2,1)S(1)} %pad_maximum_fusion.6), channel_id=1, source_target_pairs={{0,2},{1,3},{2,0},{3,1},{4,6},{5,7},{6,4},{7,5},{8,10},{9,11},{10,... | collective-permute-start | bytes 1671176 | tf_op jit(solution)/shard_map/ppermute | solution.py:32
  43.6 1.3 copy-start.12
  43.6 1.4 copy-start.13
  44.8 2.6 %copy-start.31 = (s32[16]{0:T(128)S(1)}, s32[16]{0:T(128)}, u32[]{:S(2)}) copy-start(s32[16]{0:T(128)} %param.14) | copy-start | bytes 196
  44.8 3.9 %collective-permute-start.7 = (bf16[2,2,2,32,2048]{4,3,2,1,0:T(8,128)(2,1)}, bf16[2,2,2,32,2048]{4,3,2,1,0:T(8,128)(2,1)}, u32[]{:S(2)}, u32[]{:S(2)}) collective-permute-start(bf16[2,2,2,32,2048]{4,3,2,1,0:T(8,128)(2,1)} %pad_maximum_fusion.5), channel_id=1, source_target_pairs={{0,1},{1,0},{2,3},{3,2},{4,5},{5,4},{6,7},{7,6},{8,9},{9,8},{10,11... | collective-permute-start | bytes 3145736 | tf_op jit(solution)/shard_map/ppermute | solution.py:32
  45.0 0.8 copy-start.8
  45.0 1.9 copy-start.10
  46.9 5.0 %collective-permute-start.3 = (bf16[2,2,2,32,2176]{4,3,2,1,0:T(8,128)(2,1)}, bf16[2,2,2,32,2176]{4,3,2,1,0:T(8,128)(2,1)}, u32[]{:S(2)}, u32[]{:S(2)}) collective-permute-start(bf16[2,2,2,32,2176]{4,3,2,1,0:T(8,128)(2,1)} %pad_maximum_fusion.4), channel_id=1, source_target_pairs={{0,1},{1,0},{2,3},{3,2},{4,5},{5,4},{6,7},{7,6},{8,9},{9,8},{10,11... | collective-permute-start | bytes 3342344 | tf_op jit(solution)/shard_map/ppermute | solution.py:32
  50.3 1.6 copy-start.9
  50.4 1.6 copy-start.11
  53.7 1.4 copy-start.2
  55.7 2.7 %copy-start.4 = (bf16[2,2,2,2,32,2048]{5,4,3,2,1,0:T(8,128)(2,1)S(1)}, bf16[2,2,2,2,32,2048]{5,4,3,2,1,0:T(8,128)(2,1)}, u32[]{:S(2)}) copy-start(bf16[2,2,2,2,32,2048]{5,4,3,2,1,0:T(8,128)(2,1)} %pad_maximum_fusion.2) | copy-start | bytes 6291460
  58.5 1.9 copy-start.30
  60.4 3.9 %copy-start.21 = (bf16[384,2048]{1,0:T(8,128)(2,1)}, bf16[384,2048]{1,0:T(8,128)(2,1)S(1)}, u32[]{:S(2)}) copy-start(bf16[384,2048]{1,0:T(8,128)(2,1)S(1)} %convolution_convert_fusion.5) | copy-start | bytes 4718596
  60.4 2.5 %copy-start.29 = (bf16[1,2048,768]{2,1,0:T(8,128)(2,1)S(1)}, bf16[1,2048,768]{2,1,0:T(8,128)(2,1)}, u32[]{:S(2)}) copy-start(bf16[1,2048,768]{2,1,0:T(8,128)(2,1)} %param.12) | copy-start | bytes 9437188
  67.0 3.1 %copy-start.14 = (bf16[384,768]{1,0:T(8,128)(2,1)}, bf16[384,768]{1,0:T(8,128)(2,1)S(1)}, u32[]{:S(2)}) copy-start(bf16[384,768]{1,0:T(8,128)(2,1)S(1)} %get-tuple-element.26) | copy-start | bytes 1769476
  70.1 103.3 %collective-permute-start.19 = (bf16[384,768]{1,0:T(8,128)(2,1)}, bf16[384,768]{1,0:T(8,128)(2,1)}, u32[]{:S(2)}, u32[]{:S(2)}) collective-permute-start(bf16[384,768]{1,0:T(8,128)(2,1)} %get-tuple-element.14), channel_id=1, source_target_pairs={{0,8},{1,9},{2,10},{3,11},{4,12},{5,13},{6,14},{7,15},{8,0},{9,1},... | collective-permute-start | bytes 1769480 | tf_op jit(solution)/shard_map/ppermute | solution.py:125
  79.6 25.1 %collective-permute-start.12 = (bf16[8,32,2048]{2,1,0:T(8,128)(2,1)}, bf16[8,32,2048]{2,1,0:T(8,128)(2,1)}, u32[]{:S(2)}, u32[]{:S(2)}) collective-permute-start(bf16[8,32,2048]{2,1,0:T(8,128)(2,1)} %select_bitcast_fusion.2), channel_id=1, source_target_pairs={{0,1},{1,0},{2,3},{3,2},{4,5},{5,4},{6,7},{7,6},{8,9},{9,8},{10,11... | collective-permute-start | bytes 3145736 | tf_op jit(solution)/shard_map/ppermute | solution.py:32
  82.2 1.4 copy-start.23
  83.6 1.4 copy-start.5
  83.6 2.5 %copy-start.3 = (bf16[2,2,2,2,32,2176]{5,4,3,2,1,0:T(8,128)(2,1)S(1)}, bf16[2,2,2,2,32,2176]{5,4,3,2,1,0:T(8,128)(2,1)}, u32[]{:S(2)}) copy-start(bf16[2,2,2,2,32,2176]{5,4,3,2,1,0:T(8,128)(2,1)} %copy-done.2) | copy-start | bytes 6684676
  87.8 20.0 %collective-permute-start.8 = (bf16[8,32,2048]{2,1,0:T(8,128)(2,1)}, bf16[8,32,2048]{2,1,0:T(8,128)(2,1)}, u32[]{:S(2)}, u32[]{:S(2)}) collective-permute-start(bf16[8,32,2048]{2,1,0:T(8,128)(2,1)} %select_bitcast_fusion.3), channel_id=1, source_target_pairs={{0,1},{1,0},{2,3},{3,2},{4,5},{5,4},{6,7},{7,6},{8,9},{9,8},{10,11... | collective-permute-start | bytes 3145736 | tf_op jit(solution)/shard_map/ppermute | solution.py:32
  98.4 1.5 copy-start.15
  98.4 1.7 copy-start.17
  100.1 4.7 %copy-start.7 = (bf16[512,2048]{1,0:T(8,128)(2,1)S(1)}, bf16[512,2048]{1,0:T(8,128)(2,1)}, u32[]{:S(2)}) copy-start(bf16[512,2048]{1,0:T(8,128)(2,1)} %convolution_convert_fusion.1) | copy-start | bytes 6291460
  100.2 90.0 %collective-permute-start.16 = (bf16[512,2176]{0,1:T(8,128)(2,1)}, bf16[512,2176]{0,1:T(8,128)(2,1)}, u32[]{:S(2)}, u32[]{:S(2)}) collective-permute-start(bf16[512,2176]{0,1:T(8,128)(2,1)} %pad_maximum_fusion.1), channel_id=1, source_target_pairs={{0,16},{16,0},{1,17},{17,1},{2,18},{18,2},{3,19},{19,3},{4,20},{20... | collective-permute-start | bytes 6684680 | tf_op jit(solution)/shard_map/ppermute | solution.py:163
  101.8 6.0 %copy-start.6 = (bf16[512,2048]{1,0:T(8,128)(2,1)S(1)}, bf16[512,2048]{1,0:T(8,128)(2,1)}, u32[]{:S(2)}) copy-start(bf16[512,2048]{1,0:T(8,128)(2,1)} %copy-done.5) | copy-start | bytes 6291460
  101.8 74.8 %collective-permute-start.17 = (bf16[384,1536]{1,0:T(8,128)(2,1)S(1)}, bf16[384,1536]{1,0:T(8,128)(2,1)S(1)}, u32[]{:S(2)}, u32[]{:S(2)}) collective-permute-start(bf16[384,1536]{1,0:T(8,128)(2,1)S(1)} %pad_maximum_fusion.3), channel_id=1, source_target_pairs={{0,8},{1,9},{2,10},{3,11},{4,12},{5,13},{6,14},{7,15},{8,0},{9,1},... | collective-permute-start | bytes 3538952 | tf_op jit(solution)/shard_map/ppermute | solution.py:127
  106.6 14.9 %collective-permute-start.13 = (bf16[4,32,2048]{2,1,0:T(8,128)(2,1)S(1)}, bf16[4,32,2048]{2,1,0:T(8,128)(2,1)S(1)}, u32[]{:S(2)}, u32[]{:S(2)}) collective-permute-start(bf16[4,32,2048]{2,1,0:T(8,128)(2,1)S(1)} %select_bitcast_fusion.8), channel_id=1, source_target_pairs={{0,2},{1,3},{2,0},{3,1},{4,6},{5,7},{6,4},{7,5},{8,10},{9,11},{10,... | collective-permute-start | bytes 1572872 | tf_op jit(solution)/shard_map/ppermute | solution.py:32
  109.6 21.6 %collective-permute-start.9 = (bf16[4,32,2048]{2,1,0:T(8,128)(2,1)S(1)}, bf16[4,32,2048]{2,1,0:T(8,128)(2,1)S(1)}, u32[]{:S(2)}, u32[]{:S(2)}) collective-permute-start(bf16[4,32,2048]{2,1,0:T(8,128)(2,1)S(1)} %fusion.61), channel_id=1, source_target_pairs={{0,2},{1,3},{2,0},{3,1},{4,6},{5,7},{6,4},{7,5},{8,10},{9,11},{10,... | collective-permute-start | bytes 1572872 | tf_op jit(solution)/shard_map/ppermute | solution.py:32
  121.8 15.0 %collective-permute-start.14 = (bf16[2,32,2048]{2,1,0:T(8,128)(2,1)S(1)}, bf16[2,32,2048]{2,1,0:T(8,128)(2,1)S(1)}, u32[]{:S(2)}, u32[]{:S(2)}) collective-permute-start(bf16[2,32,2048]{2,1,0:T(8,128)(2,1)S(1)} %select_bitcast_fusion.13), channel_id=1, source_target_pairs={{0,4},{1,5},{2,6},{3,7},{4,0},{5,1},{6,2},{7,3},{8,12},{9,13},{10,... | collective-permute-start | bytes 786440 | tf_op jit(solution)/shard_map/ppermute | solution.py:32
  131.5 32.1 %collective-permute-start.10 = (bf16[2,32,2048]{2,1,0:T(8,128)(2,1)S(1)}, bf16[2,32,2048]{2,1,0:T(8,128)(2,1)S(1)}, u32[]{:S(2)}, u32[]{:S(2)}) collective-permute-start(bf16[2,32,2048]{2,1,0:T(8,128)(2,1)S(1)} %fusion.77), channel_id=1, source_target_pairs={{0,4},{1,5},{2,6},{3,7},{4,0},{5,1},{6,2},{7,3},{8,12},{9,13},{10,... | collective-permute-start | bytes 786440 | tf_op jit(solution)/shard_map/ppermute | solution.py:32
  137.0 39.7 %copy-start.22 = (bf16[384,2048]{1,0:T(8,128)(2,1)S(1)}, bf16[384,2048]{1,0:T(8,128)(2,1)}, u32[]{:S(2)}) copy-start(bf16[384,2048]{1,0:T(8,128)(2,1)} %copy-done.21) | copy-start | bytes 4718596
  137.0 39.7 %copy-start.24 = (bf16[384,2048]{1,0:T(8,128)(2,1)S(1)}, bf16[384,2048]{1,0:T(8,128)(2,1)}, u32[]{:S(2)}) copy-start(bf16[384,2048]{1,0:T(8,128)(2,1)} %copy-done.23) | copy-start | bytes 4718596
  137.0 29.2 %collective-permute-start.15 = (bf16[1,32,2048]{2,1,0:T(8,128)(2,1)S(1)}, bf16[1,32,2048]{2,1,0:T(8,128)(2,1)S(1)}, u32[]{:S(2)}, u32[]{:S(2)}) collective-permute-start(bf16[1,32,2048]{2,1,0:T(8,128)(2,1)S(1)} %select_bitcast_fusion.18), channel_id=1, source_target_pairs={{0,8},{1,9},{2,10},{3,11},{4,12},{5,13},{6,14},{7,15},{8,0},{9,1},... | collective-permute-start | bytes 393224 | tf_op jit(solution)/shard_map/ppermute | solution.py:32
  163.8 8.9 %collective-permute-start.11 = (bf16[1,32,2048]{2,1,0:T(8,128)(2,1)S(1)}, bf16[1,32,2048]{2,1,0:T(8,128)(2,1)S(1)}, u32[]{:S(2)}, u32[]{:S(2)}) collective-permute-start(bf16[1,32,2048]{2,1,0:T(8,128)(2,1)S(1)} %select_bitcast_fusion.19), channel_id=1, source_target_pairs={{0,8},{1,9},{2,10},{3,11},{4,12},{5,13},{6,14},{7,15},{8,0},{9,1},... | collective-permute-start | bytes 393224 | tf_op jit(solution)/shard_map/ppermute | solution.py:32
  173.4 9.9 %copy-start.16 = (bf16[384,768]{1,0:T(8,128)(2,1)S(1)}, bf16[384,768]{1,0:T(8,128)(2,1)}, u32[]{:S(2)}) copy-start(bf16[384,768]{1,0:T(8,128)(2,1)} %copy-done.14) | copy-start | bytes 1769476
  173.4 9.9 %copy-start.18 = (bf16[384,768]{1,0:T(8,128)(2,1)S(1)}, bf16[384,768]{1,0:T(8,128)(2,1)}, u32[]{:S(2)}) copy-start(bf16[384,768]{1,0:T(8,128)(2,1)} %get-tuple-element.27) | copy-start | bytes 1769476
  175.4 23.5 %collective-permute-start.20 = (bf16[384,768]{1,0:T(8,128)(2,1)}, bf16[384,768]{1,0:T(8,128)(2,1)}, u32[]{:S(2)}, u32[]{:S(2)}) collective-permute-start(bf16[384,768]{1,0:T(8,128)(2,1)} %broadcast_select_fusion.1), channel_id=1, source_target_pairs={{0,16},{16,0},{1,17},{17,1},{2,18},{18,2},{3,19},{19,3},{4,20},{20... | collective-permute-start | bytes 1769480 | tf_op jit(solution)/shard_map/ppermute | solution.py:164
  176.6 1.0 copy-start.25
  177.7 11.9 %copy-start.28 = (s32[32,8]{0,1:T(8,128)S(1)}, s32[32,8]{0,1:T(8,128)}, u32[]{:S(2)}) copy-start(s32[32,8]{0,1:T(8,128)} %param.9) | copy-start | bytes 3076
  178.5 11.1 %all-to-all-start = ((f32[16,1,32]{2,1,0:T(1,128)}), f32[16,1,32]{2,1,0:T(1,128)S(1)}, u32[]{:S(2)}, u32[]{:S(2)}) async-start(f32[16,1,32]{2,1,0:T(1,128)} %bitcast.61), calls=%async_computation | async-start | bytes 16384 | tf_op jit(solution)/shard_map/all_to_all | solution.py:139
  184.8 9.5 %copy-start.26 = (bf16[384,1536]{1,0:T(8,128)(2,1)}, bf16[384,1536]{1,0:T(8,128)(2,1)S(1)}, u32[]{:S(2)}) copy-start(bf16[384,1536]{1,0:T(8,128)(2,1)S(1)} %broadcast_select_fusion) | copy-start | bytes 3538948
  184.8 29.9 %collective-permute-start.18 = (bf16[384,1536]{1,0:T(8,128)(2,1)S(1)}, bf16[384,1536]{1,0:T(8,128)(2,1)}, u32[]{:S(2)}, u32[]{:S(2)}) collective-permute-start(bf16[384,1536]{1,0:T(8,128)(2,1)S(1)} %broadcast_select_fusion), channel_id=1, source_target_pairs={{0,16},{16,0},{1,17},{17,1},{2,18},{18,2},{3,19},{19,3},{4,20},{20... | collective-permute-start | bytes 3538952 | tf_op jit(solution)/shard_map/ppermute | solution.py:164
  194.4 3.4 %copy-start.19 = (bf16[384,2048]{1,0:T(8,128)(2,1)}, bf16[384,2048]{1,0:T(8,128)(2,1)S(1)}, u32[]{:S(2)}) copy-start(bf16[384,2048]{1,0:T(8,128)(2,1)S(1)} %convolution_convert_fusion.4) | copy-start | bytes 4718596
  197.5 1.1 copy-start.20
  198.9 15.8 %slice-start = ((bf16[384,2048]{1,0:T(8,128)(2,1)}), bf16[384,1024]{1,0:T(8,128)(2,1)S(1)}, s32[]{:S(2)}) async-start(bf16[384,2048]{1,0:T(8,128)(2,1)} %copy-done.19), calls=%async_computation.1 | async-start | bytes 1572864 | tf_op jit(solution)/shard_map/slice | solution.py:167
  198.9 15.8 %slice-start.1 = ((bf16[384,2048]{1,0:T(8,128)(2,1)}), bf16[384,1024]{1,0:T(8,128)(2,1)S(1)}, s32[]{:S(2)}) async-start(bf16[384,2048]{1,0:T(8,128)(2,1)} %copy-done.20), calls=%async_computation.2 | async-start | bytes 1572864 | tf_op jit(solution)/shard_map/slice | solution.py:167
  198.9 15.8 %copy-start.27 = (bf16[384,1536]{1,0:T(8,128)(2,1)S(1)}, bf16[384,1536]{1,0:T(8,128)(2,1)}, u32[]{:S(2)}) copy-start(bf16[384,1536]{1,0:T(8,128)(2,1)} %copy-done.26) | copy-start | bytes 3538948
  214.7 6.2 %copy-start.1 = (bf16[1,768,2048]{2,1,0:T(8,128)(2,1)S(1)}, bf16[1,768,2048]{2,1,0:T(8,128)(2,1)}, u32[]{:S(2)}) copy-start(bf16[1,768,2048]{2,1,0:T(8,128)(2,1)} %param.13) | copy-start | bytes 9437188
